TPU v7x, 32 devices: a whole 2x2x4 slice. The times are simulated.
32 devices in a mesh: group: 2 (over x), seq: 4 (over y, core), tp: 4 (over z).
Axes of the slice: x: 2, y: 2, z: 4, core: 2. Of those that a mesh axis runs over, the one named last changes fastest.
Arguments:
- queries: bfloat16 [4096, 4096], P(('group', 'seq'), 'tp'), parts along dimension 0, may hold values from -32 to 32
- key_value: bfloat16 [4096, 2, 2048], P(('group', 'seq'), None, 'tp'), parts along dimension 0, may hold values from -32 to 32
- window_cache: bfloat16 [2048, 2, 2048], P('group', None, 'tp'), parts along dimension 0, may hold values from -5 to 5
- span_start: int32 [2], P('group'), parts along dimension 0, may hold values from 1024 to 30720
- hidden: bfloat16 [4096, 21504], P(('group', 'seq'), 'tp'), parts along dimension 0, may hold values from -6 to 6
- down_codes: int32 [21504, 2688], P('tp', 'seq'), may hold values from 0 to 15
- down_scales: int32 [168, 2688], P('tp', 'seq'), may hold values from 1 to 15
- out_weight: bfloat16 [4096, 2688], P('tp', 'seq'), may hold values from -0.375 to 0.375
Outputs:
- layer_update: bfloat16 [4096, 2688], P(('group', 'seq', 'tp')), parts along dimension 0
There are 2 independent parts, one for each index of `group`. A program takes and returns all parts, laid end to end along the dimension named above; an argument that names none is the same for every part. Nothing has to cross between parts.
All inputs are finite; a program needn't handle non-finite values.
Results may differ from a plain program's by a relative error of at most 0.02.
Values may be sent and summed in bfloat16 or wider, within the bound.
A program may use at most 192 MiB of HBM per device.

v0:
```python
import jax
import jax.numpy as jnp
import numpy as np
from jax import lax
from jax.sharding import PartitionSpec as P

HD = 128
WINDOW = 1024
GROUP = 128


ROPE_BASE = 10000.0
SCORE_SCALE = 168.0 ** (-0.5)
CODE_STEP = 2.0 ** (-14)
INV_ROOT = 1344.0 ** (-0.5)


def shifted(value, axis, steps):
    count = lax.axis_size(axis)
    first, last = (max(0, -steps), min(count, count - steps))
    return lax.ppermute(value, axis, [(source, source + steps) for source in range(first, last)])


def swapped(x, axis, stride):
    return lax.ppermute(x, axis, [(i, i ^ 1 << stride) for i in range(lax.axis_size(axis))])


def bit_total(value_now):
    return (value_now & 1) + (value_now >> 1 & 1) + (value_now >> 2 & 1)


def build_tables():
    prime_order = 167
    residues = set((value_now * value_now % prime_order for value_now in range(1, prime_order)))
    legendre = [0] + [1 if value_now in residues else -1 for value_now in range(1, prime_order)]
    paley_table = np.eye(prime_order + 1)
    paley_table[0, 1:] += 1.0
    paley_table[1:, 0] -= 1.0
    for row_index in range(prime_order):
        for col_index in range(prime_order):
            paley_table[row_index + 1, col_index + 1] += legendre[
                (col_index - row_index) % prime_order
            ]
    sylvester = np.array(
        [
            [(-1.0) ** bit_total(left_bit & right_bit) for right_bit in range(8)]
            for left_bit in range(8)
        ]
    )
    return (paley_table, sylvester)


def rotary(values, cosine, sine_part):
    half_dim = values.shape[-1] // 2
    first_half = values[..., :half_dim]
    second_half = values[..., half_dim:]
    return jnp.concatenate(
        [
            first_half * cosine - second_half * sine_part,
            second_half * cosine + first_half * sine_part,
        ],
        axis=-1,
    )


def section_pairs(blocks_now, section_level):
    row_count, block_count, width_cols = blocks_now.shape
    paired = blocks_now.reshape(
        row_count, block_count >> section_level + 1, 2, 1 << section_level, width_cols
    ).astype(jnp.float32)
    upper_half = paired[:, :, 0]
    lower_half = paired[:, :, 1]
    mixed = jnp.stack([upper_half + lower_half, upper_half - lower_half], axis=2)
    return mixed.astype(jnp.bfloat16).reshape(row_count, block_count, width_cols)


def per_device(
    queries, key_value, window_cache, span_start, hidden, down_codes, down_scales, out_weight
):
    tok_rows = queries.shape[0]
    tp_count = lax.axis_size("tp")
    seq_index = lax.axis_index("seq")
    tp_index = lax.axis_index("tp")
    heads_dev = queries.shape[1] // HD
    kv_dev = key_value.shape[2] // HD
    group_size = heads_dev // kv_dev
    first_pos = span_start[0]
    positions = first_pos + seq_index * tok_rows + jnp.arange(tok_rows, dtype=jnp.int32)
    inv_freq = ROPE_BASE ** (-(2.0 * jnp.arange(HD // 2, dtype=jnp.float32)) / HD)
    angles = positions.astype(jnp.float32)[:, None] * inv_freq[None, :]
    cosine = jnp.cos(angles)[:, None, :]
    sine_part = jnp.sin(angles)[:, None, :]
    query_rot = rotary(
        queries.reshape(tok_rows, heads_dev, HD).astype(jnp.float32), cosine, sine_part
    ).astype(jnp.bfloat16)
    key_rot = rotary(
        key_value[:, 0].reshape(tok_rows, kv_dev, HD).astype(jnp.float32), cosine, sine_part
    ).astype(jnp.bfloat16)
    own_pairs = jnp.stack([key_rot.reshape(tok_rows, kv_dev * HD), key_value[:, 1]], axis=1)
    reach_blocks = WINDOW // tok_rows
    earlier = []
    moving = own_pairs
    for hop_count in range(reach_blocks):
        moving = shifted(moving, "seq", 1)
        earlier.insert(0, moving)
    halo_rows = jnp.concatenate(earlier, axis=0)
    doubled = jnp.concatenate([window_cache, window_cache], axis=0)
    ordered = lax.dynamic_slice_in_dim(doubled, first_pos % WINDOW, WINDOW, 0)
    padded_cache = jnp.concatenate([ordered, jnp.zeros_like(ordered)], axis=0)
    from_cache = lax.dynamic_slice_in_dim(
        padded_cache, jnp.minimum(seq_index * tok_rows, WINDOW), WINDOW, 0
    )
    halo_rows = halo_rows + from_cache
    all_rows = jnp.concatenate([halo_rows, own_pairs], axis=0)
    key_count = all_rows.shape[0]
    key_rows = all_rows[:, 0].reshape(key_count, kv_dev, HD)
    value_rows = all_rows[:, 1].reshape(key_count, kv_dev, HD)
    grouped = query_rot.reshape(tok_rows, kv_dev, group_size, HD)
    scores = (
        jnp.einsum("qkgd,skd->kgqs", grouped, key_rows, preferred_element_type=jnp.float32)
        * SCORE_SCALE
    )
    query_ids = jnp.arange(tok_rows)[:, None]
    key_ids = jnp.arange(key_count)[None, :]
    allowed = (key_ids > query_ids) & (key_ids <= query_ids + WINDOW)
    scores = jnp.where(allowed, scores, -jnp.inf)
    top_score = jnp.max(scores, axis=-1, keepdims=True)
    weights_soft = jnp.exp(scores - top_score)
    weights_soft = (weights_soft / jnp.sum(weights_soft, axis=-1, keepdims=True)).astype(
        jnp.bfloat16
    )
    attended = jnp.einsum(
        "kgqs,skd->qkgd", weights_soft, value_rows, preferred_element_type=jnp.float32
    )
    attended = attended.astype(jnp.bfloat16).reshape(tok_rows, heads_dev * HD)
    paley_np, sylvester_np = build_tables()
    paley_table = jnp.asarray(paley_np, dtype=jnp.bfloat16)
    sylvester = jnp.asarray(sylvester_np, dtype=jnp.float32)
    local_blocks = hidden.shape[1] // 1344
    local_levels = local_blocks.bit_length() - 1
    parts_now = hidden.reshape(tok_rows, local_blocks, 8, 168)
    mixed = jnp.einsum("nbac,cd->nbad", parts_now, paley_table, preferred_element_type=jnp.float32)
    mixed = (
        jnp.einsum("nbad,ae->nbed", mixed, sylvester, precision=lax.Precision.HIGHEST) * INV_ROOT
    )
    blocks_now = mixed.reshape(tok_rows, local_blocks, 1344).astype(jnp.bfloat16)
    for section_level in range(local_levels):
        blocks_now = section_pairs(blocks_now, section_level)
    for bit_index in range(tp_count.bit_length() - 1):
        partner = swapped(blocks_now, "tp", bit_index)
        high_side = jnp.right_shift(tp_index, bit_index) % 2
        own_values = blocks_now.astype(jnp.float32)
        other_values = partner.astype(jnp.float32)
        blocks_now = jnp.where(
            high_side == 0, own_values + other_values, other_values - own_values
        ).astype(jnp.bfloat16)
    rotated = blocks_now.reshape(tok_rows, local_blocks * 1344)
    joined = jnp.concatenate([rotated, attended], axis=1)
    group_count = down_scales.shape[0]
    col_count = down_codes.shape[1]
    down_weight = (
        (down_codes.reshape(group_count, GROUP, col_count) - 8) * down_scales[:, None, :]
    ).astype(jnp.float32) * CODE_STEP
    down_rows = down_weight.astype(jnp.bfloat16).reshape(group_count * GROUP, col_count)
    stacked = jnp.concatenate([down_rows, out_weight], axis=0)
    partials = jnp.dot(
        joined,
        lax.all_gather(stacked, "seq", axis=1, tiled=True),
        preferred_element_type=jnp.float32,
    )
    layer_update = lax.psum_scatter(
        partials.astype(jnp.bfloat16), "tp", scatter_dimension=0, tiled=True
    )
    return layer_update


def solution(mesh):
    return jax.shard_map(
        per_device,
        mesh=mesh,
        in_specs=(
            P(("group", "seq"), "tp"),
            P(("group", "seq"), None, "tp"),
            P("group", None, "tp"),
            P("group"),
            P(("group", "seq"), "tp"),
            P("tp", "seq"),
            P("tp", "seq"),
            P("tp", "seq"),
        ),
        out_specs=P(("group", "seq", "tp"), None),
        check_vma=False,
    )
```

profile of v0, /device:TPU:0, one launch (start us, length us, event | category | flops | bytes accessed | tf_op | source)
XLA Modules:
  0.0 548.5 jit_solution(3099437337702410601)
XLA Ops:
  7.6 4.5 mul.147
  12.2 9.4 %fusion.4 = bf16[5376,672]{0,1:T(8,128)(2,1)S(1)} fusion(s32[84,8,42,128]{3,2,1,0:T(8,128)S(1)} %bitcast.77, s32[5376,672]{0,1:T(8,128)} %param.15), kind=kLoop, calls=%fused_computation.8 | loop fusion | flops 18063360 | bytes 36126720 | tf_op jit(solution)/shard_map/convert_element_type | solution.py:164
  21.6 3.7 pad_maximum_fusion
  25.5 8.3 %copy.33 = bf16[512,5376]{0,1:T(8,128)(2,1)} copy(bf16[512,5376]{1,0:T(8,128)(2,1)} %param.14) | data formatting | bytes 11010048 | tf_op args[4]
  33.8 5.6 %convolution_bitcast_fusion = f32[512,4,8,168]{0,3,2,1:T(8,128)S(1)} fusion(bf16[168,168,1,1]{0,1,3,2:T(8,128)(2,1)S(1)} %copy-done.7, bf16[512,4,8,168]{0,3,2,1:T(8,128)(2,1)} %bitcast.79), kind=kOutput, calls=%fused_computation.43 | convolution fusion | flops 924844032 | bytes 16571520 | tf_op jit(solution)/shard_map/nbac,cd->nbad/dot_general | solution.py:142
  39.4 16.7 %convert_bitcast_fusion = f32[512,4,8,168]{0,2,3,1:T(8,128)} fusion(f32[8,8,1,1]{0,1,3,2:T(8,128)S(1)} %copy-done.8, f32[512,4,8,168]{0,3,2,1:T(8,128)S(1)} %convolution_bitcast_fusion), kind=kOutput, calls=%fused_computation.23 | convolution fusion | flops 272498688 | bytes 22020352 | tf_op jit(solution)/shard_map/nbad,ae->nbed/dot_general | solution.py:144
  56.2 11.1 %copy.35 = f32[512,4,8,168]{0,3,2,1:T(8,128)S(1)} copy(f32[512,4,8,168]{0,2,3,1:T(8,128)} %convert_bitcast_fusion) | data formatting | bytes 22020096 | tf_op jit(solution)/shard_map/convert_element_type | solution.py:70
  67.2 4.1 fusion.27
  71.3 3.3 maximum_convert_fusion
  74.6 1.9 add_convert_fusion
  77.0 2.7 copy.37
  79.8 3.3 collective-permute-start
  83.8 2.5 fusion.45
  86.7 2.3 copy.60
  89.9 2.5 collective-permute-start.2
  92.4 109.7 %collective-permute-done = bf16[512,4,1344]{0,2,1:T(8,128)(2,1)} collective-permute-done((bf16[512,4,1344]{0,2,1:T(8,128)(2,1)}, bf16[512,4,1344]{0,2,1:T(8,128)(2,1)}, u32[]{:S(2)}, u32[]{:S(2)}) %collective-permute-start) | collective-permute-done | bytes 5505056 | tf_op jit(solution)/shard_map/ppermute | solution.py:25
  202.1 8.6 %fusion.10 = bf16[512,4,1344]{0,2,1:T(8,128)(2,1)} fusion(bf16[512,4,1344]{0,2,1:T(8,128)(2,1)} %collective-permute-done, pred[]{:T(512)S(6)} %eq.11, bf16[512,1,2,2,1344]{0,4,3,2,1:T(8,128)(2,1)} %copy.37), kind=kLoop, calls=%fused_computation.18 | loop fusion | flops 16515072 | bytes 16515073 | tf_op jit(solution)/shard_map/convert_element_type | solution.py:156
  210.7 2.8 collective-permute-start.1
  214.2 2.7 fusion.44
  216.9 2.2 collective-permute-start.3
  220.1 4.7 copy.42
  224.9 2.1 fusion.30
  227.1 1.8 subtract_convert_fusion.2
  228.9 1.6 fusion.26
  230.5 2.7 fusion.29
  233.7 12.0 %fusion.32 = f32[4,1536,512,2]{2,1,3,0:T(8,128)} fusion(bf16[1536,4,128,1]{0,2,3,1:T(8,128)(2,1)S(1)} %bitcast.81, bf16[512,4,2,64]{3,0,2,1:T(8,128)(2,1)S(1)} %bitcast.88, bf16[512,4,2,64]{3,0,2,1:T(8,128)(2,1)S(1)} %bitcast.86), kind=kOutput, calls=%fused_computation.62 | convolution fusion | flops 1612709888 | bytes 27787264 | tf_op jit(solution)/shard_map/qkgd,skd->kgqs/dot_general | solution.py:120
  245.7 10.3 %fusion.46 = f32[4,2,512]{2,1,0:T(2,128)S(1)} fusion(pred[512,1536]{0,1:T(8,128)(4,1)} %fusion.26, bf16[1536,4,128,1]{0,2,3,1:T(8,128)(2,1)S(1)} %bitcast.82, bf16[512,4,2,64]{3,0,2,1:T(8,128)(2,1)} %bitcast.89, bf16[512,4,2,64]{3,0,2,1:T(8,128)(2,1)} %bitcast.87), kind=kOutput, calls=%fused_computation.76 | convolution fusion | flops 1637877248 | bytes 3424256 | tf_op jit(solution)/shard_map/sub | solution.py:128
  256.0 13.2 %fusion.31 = bf16[4,128,2,512]{3,1,2,0:T(8,128)(2,1)S(1)} fusion(bf16[1536,4,128,1]{0,2,3,1:T(8,128)(2,1)S(1)} %bitcast.91, f32[4,2,512]{2,1,0:T(2,128)S(1)} %fusion.46, f32[4,1536,512,2]{2,1,3,0:T(8,128)} %fusion.32, pred[512,1536]{0,1:T(8,128)(4,1)} %fusion.26), kind=kOutput, calls=%fused_computation.53 | convolution fusion | flops 1642599936 | bytes 28590080 | tf_op jit(solution)/shard_map/kgqs,skd->qkgd/dot_general | solution.py:132
  269.2 180.5 %collective-permute-done.1 = bf16[512,4,1344]{0,2,1:T(8,128)(2,1)} collective-permute-done((bf16[512,4,1344]{0,2,1:T(8,128)(2,1)}, bf16[512,4,1344]{0,2,1:T(8,128)(2,1)}, u32[]{:S(2)}, u32[]{:S(2)}) %collective-permute-start.1) | collective-permute-done | bytes 5505056 | tf_op jit(solution)/shard_map/ppermute | solution.py:25
  449.7 8.6 %fusion.12 = bf16[512,4,1344]{0,2,1:T(8,128)(2,1)} fusion(bf16[512,4,1344]{0,2,1:T(8,128)(2,1)} %collective-permute-done.1, bf16[512,4,1344]{0,2,1:T(8,128)(2,1)} %fusion.10, pred[]{:T(512)S(6)} %eq.10), kind=kLoop, calls=%fused_computation.20 | loop fusion | flops 16515072 | bytes 16515073 | tf_op jit(solution)/shard_map/convert_element_type | solution.py:156
  458.3 27.9 %fusion.19 = bf16[512,2688]{1,0:T(8,128)(2,1)} fusion(bf16[6400,2688]{0,1:T(8,128)(2,1)} %all-gather.2.cloned.1.call-done, bf16[512,1024]{0,1:T(8,128)(2,1)S(1)} %bitcast.92, bf16[512,5376]{0,1:T(8,128)(2,1)} %bitcast.83), kind=kOutput, calls=%fused_computation.38 | convolution fusion | flops 17630560256 | bytes 43712512 | tf_op jit(solution)/shard_map/dot_general | solution.py:166
  486.3 55.1 %reduce-scatter.2.cloned.1.call-done = bf16[128,2688]{1,0:T(8,128)(2,1)} async-done(((bf16[512,2688]{1,0:T(8,128)(2,1)}), bf16[128,2688]{1,0:T(8,128)(2,1)}) %reduce-scatter.2.cloned.1.call-update) | async-done | bytes 688144 | tf_op jit(solution)/shard_map/reduce_scatter | solution.py:171
  (42 shorter events, 5.3 us)
Async XLA Ops:
  6.5 451.8 %all-gather.2.cloned.1.call-start = ((), (), s32[]{:S(2)}) async-start(), calls=%async_computation.1 | async-start | bytes 43008000 | tf_op jit(solution)/shard_map/all_gather | solution.py:168
  12.2 9.4 %copy-start.5 = (bf16[1024,672]{0,1:T(8,128)(2,1)S(1)}, bf16[1024,672]{0,1:T(8,128)(2,1)}, u32[]{:S(2)}) copy-start(bf16[1024,672]{0,1:T(8,128)(2,1)} %param.17) | copy-start | bytes 4128772
  25.3 8.5 %copy-start.7 = (bf16[168,168,1,1]{0,1,3,2:T(8,128)(2,1)S(1)}, bf16[168,168,1,1]{0,1,3,2:T(8,128)(2,1)}, u32[]{:S(2)}) copy-start(bf16[168,168,1,1]{0,1,3,2:T(8,128)(2,1)} %constant.73) | copy-start | bytes 169348
  25.3 516.1 %reduce-scatter.2.cloned.1.call-start = ((), (), s32[]{:S(2)}) async-start(), calls=%async_computation.2 | async-start | bytes 3440640 | tf_op jit(solution)/shard_map/reduce_scatter | solution.py:171
  33.8 5.6 %copy-start.8 = (f32[8,8,1,1]{0,1,3,2:T(8,128)S(1)}, f32[8,8,1,1]{0,1,3,2:T(8,128)}, u32[]{:S(2)}) copy-start(f32[8,8,1,1]{0,1,3,2:T(8,128)} %constant.74) | copy-start | bytes 772
  77.0 6.7 %copy-start.4 = (bf16[512,2,512]{2,1,0:T(2,128)(2,1)S(1)}, bf16[512,2,512]{2,1,0:T(2,128)(2,1)}, u32[]{:S(2)}) copy-start(bf16[512,2,512]{2,1,0:T(2,128)(2,1)} %param.11) | copy-start | bytes 3145732
  79.8 122.3 %collective-permute-start = (bf16[512,4,1344]{0,2,1:T(8,128)(2,1)}, bf16[512,4,1344]{0,2,1:T(8,128)(2,1)}, u32[]{:S(2)}, u32[]{:S(2)}) collective-permute-start(bf16[512,4,1344]{0,2,1:T(8,128)(2,1)} %bitcast.11), channel_id=1, source_target_pairs={{0,1},{1,0},{2,3},{3,2},{4,5},{5,4},{6,7},{7,6},{8,9},{9,8},{10,11... | collective-permute-start | bytes 16515080 | tf_op jit(solution)/shard_map/ppermute | solution.py:25
  89.9 127.0 %collective-permute-start.2 = (bf16[512,2,512]{0,2,1:T(8,128)(2,1)S(1)}, bf16[512,2,512]{0,2,1:T(8,128)(2,1)}, u32[]{:S(2)}, u32[]{:S(2)}) collective-permute-start(bf16[512,2,512]{0,2,1:T(8,128)(2,1)S(1)} %pad_maximum_fusion.2), channel_id=1, source_target_pairs={{0,4},{4,8},{8,12},{1,5},{5,9},{9,13},{2,6},{6,10},{10,14},{3,7},{... | collective-permute-start | bytes 3145736 | tf_op jit(solution)/shard_map/ppermute | solution.py:21
  92.4 121.0 %copy-start.6 = (bf16[512,1024]{1,0:T(8,128)(2,1)S(1)}, bf16[512,1024]{1,0:T(8,128)(2,1)}, u32[]{:S(2)}) copy-start(bf16[512,1024]{1,0:T(8,128)(2,1)} %param.10) | copy-start | bytes 3145732
  210.7 239.0 %collective-permute-start.1 = (bf16[512,4,1344]{0,2,1:T(8,128)(2,1)}, bf16[512,4,1344]{0,2,1:T(8,128)(2,1)}, u32[]{:S(2)}, u32[]{:S(2)}) collective-permute-start(bf16[512,4,1344]{0,2,1:T(8,128)(2,1)} %fusion.10), channel_id=1, source_target_pairs={{0,2},{1,3},{2,0},{3,1},{4,6},{5,7},{6,4},{7,5},{8,10},{9,11},{10,... | collective-permute-start | bytes 16515080 | tf_op jit(solution)/shard_map/ppermute | solution.py:25
  216.9 13.6 %collective-permute-start.3 = (bf16[512,2,512]{0,2,1:T(8,128)(2,1)}, bf16[512,2,512]{0,2,1:T(8,128)(2,1)}, u32[]{:S(2)}, u32[]{:S(2)}) collective-permute-start(bf16[512,2,512]{0,2,1:T(8,128)(2,1)} %collective-permute-done.2), channel_id=1, source_target_pairs={{0,4},{4,8},{8,12},{1,5},{5,9},{9,13},{2,6},{6,10},{10,14},{3,7},{... | collective-permute-start | bytes 3145736 | tf_op jit(solution)/shard_map/ppermute | solution.py:21
  224.8 2.2 copy-start
  224.9 2.2 copy-start.1
  228.8 4.8 copy-start.2
  228.8 4.8 copy-start.3
Sparse Core Ops, SparseCore 0:
  25.4 228.7 all-gather.1
  486.4 54.9 reduce-scatter.1
where the time goes:
time: 552 us; the launch traced here: 548 us
  waiting for transfers between devices  345 us (62%)
  matrix products  85.8 us (16%)
  other arithmetic  49.7 us (9%)
  local copies, waits for them, and re-layouts  42 us (8%)
  between operations  14.6 us (3%)
  starting transfers between devices  11 us (2%)
    ppermute x2, waiting for transfers between devices, swapped(): lax.ppermute(x, axis, [(i, i ^ 1 << stride) for i in range(lax.axis_size(...  290 us
    reduce_scatter x1, waiting for transfers between devices, per_device(): lax.psum_scatter(partials.astype(jnp.bfloat16), 'tp', scatter_dimension=0...  55.1 us
    dot_general x1, matrix products, per_device(): jnp.dot(joined, lax.all_gather(stacked, 'seq', axis=1, tiled=True), prefe...  27.9 us
    convert_element_type x2, other arithmetic, per_device(): blocks_now = jnp.where(high_side == 0, own_values + other_values, other_v...  17.2 us
    unnamed x23, local copies, waits for them, and re-layouts  17 us
    dot_general x1, matrix products, per_device(): jnp.einsum('nbad,ae->nbed', mixed, sylvester, precision=lax.Precision.HIG...  16.7 us
    dot_general x1, matrix products, per_device(): jnp.einsum('kgqs,skd->qkgd', weights_soft, value_rows, preferred_element_...  13.2 us
    dot_general x1, matrix products, per_device(): jnp.einsum('qkgd,skd->kgqs', grouped, key_rows, preferred_element_type=jn...  12 us
  transfers between devices with their start and end apart: 6, of which 3 were waited for; matrix products, arithmetic and copies ran while one was open for 24% of the time, Pallas kernels for 0%

commit v1 on v0

--- a/solution.py
+++ b/solution.py
@@ -7,6 +7,8 @@
 HD = 128
 WINDOW = 1024
 GROUP = 128
+BLOCK = 1344
+CHUNKS = 3
 
 
 ROPE_BASE = 10000.0
@@ -25,29 +27,22 @@
     return lax.ppermute(x, axis, [(i, i ^ 1 << stride) for i in range(lax.axis_size(axis))])
 
 
-def bit_total(value_now):
-    return (value_now & 1) + (value_now >> 1 & 1) + (value_now >> 2 & 1)
+def block_mixer():
+    order = 167
+    residues = {value * value % order for value in range(1, order)}
+    legendre = np.array([0] + [1 if value in residues else -1 for value in range(1, order)])
+    paley = np.eye(order + 1)
+    paley[0, 1:] += 1
+    paley[1:, 0] -= 1
+    places = np.arange(order)
+    paley[1:, 1:] += legendre[(places[None, :] - places[:, None]) % order]
+    pair = np.array([[1, 1], [1, -1]])
+    return jnp.asarray(np.kron(np.kron(np.kron(pair, pair), pair), paley), jnp.bfloat16)
 
 
-def build_tables():
-    prime_order = 167
-    residues = set((value_now * value_now % prime_order for value_now in range(1, prime_order)))
-    legendre = [0] + [1 if value_now in residues else -1 for value_now in range(1, prime_order)]
-    paley_table = np.eye(prime_order + 1)
-    paley_table[0, 1:] += 1.0
-    paley_table[1:, 0] -= 1.0
-    for row_index in range(prime_order):
-        for col_index in range(prime_order):
-            paley_table[row_index + 1, col_index + 1] += legendre[
-                (col_index - row_index) % prime_order
-            ]
-    sylvester = np.array(
-        [
-            [(-1.0) ** bit_total(left_bit & right_bit) for right_bit in range(8)]
-            for left_bit in range(8)
-        ]
-    )
-    return (paley_table, sylvester)
+def gathered(piece):
+    wide = lax.all_gather(piece, "group", axis=0, tiled=True)
+    return lax.all_gather(wide, "seq", axis=1, tiled=True)
 
 
 def rotary(values, cosine, sine_part):
@@ -133,41 +128,49 @@
         "kgqs,skd->qkgd", weights_soft, value_rows, preferred_element_type=jnp.float32
     )
     attended = attended.astype(jnp.bfloat16).reshape(tok_rows, heads_dev * HD)
-    paley_np, sylvester_np = build_tables()
-    paley_table = jnp.asarray(paley_np, dtype=jnp.bfloat16)
-    sylvester = jnp.asarray(sylvester_np, dtype=jnp.float32)
-    local_blocks = hidden.shape[1] // 1344
-    local_levels = local_blocks.bit_length() - 1
-    parts_now = hidden.reshape(tok_rows, local_blocks, 8, 168)
-    mixed = jnp.einsum("nbac,cd->nbad", parts_now, paley_table, preferred_element_type=jnp.float32)
-    mixed = (
-        jnp.einsum("nbad,ae->nbed", mixed, sylvester, precision=lax.Precision.HIGHEST) * INV_ROOT
+    mixer = block_mixer()
+    local_blocks = hidden.shape[1] // BLOCK
+    group_index = lax.axis_index("group")
+    sides = lax.axis_size("group")
+    mixed = jnp.dot(
+        hidden.reshape(tok_rows * local_blocks, BLOCK), mixer, preferred_element_type=jnp.float32
     )
-    blocks_now = mixed.reshape(tok_rows, local_blocks, 1344).astype(jnp.bfloat16)
-    for section_level in range(local_levels):
+    blocks_now = (mixed * INV_ROOT).astype(jnp.bfloat16).reshape(tok_rows, local_blocks, BLOCK)
+    for section_level in range(local_blocks.bit_length() - 1):
         blocks_now = section_pairs(blocks_now, section_level)
-    for bit_index in range(tp_count.bit_length() - 1):
-        partner = swapped(blocks_now, "tp", bit_index)
-        high_side = jnp.right_shift(tp_index, bit_index) % 2
-        own_values = blocks_now.astype(jnp.float32)
-        other_values = partner.astype(jnp.float32)
-        blocks_now = jnp.where(
-            high_side == 0, own_values + other_values, other_values - own_values
-        ).astype(jnp.bfloat16)
-    rotated = blocks_now.reshape(tok_rows, local_blocks * 1344)
-    joined = jnp.concatenate([rotated, attended], axis=1)
-    group_count = down_scales.shape[0]
-    col_count = down_codes.shape[1]
-    down_weight = (
-        (down_codes.reshape(group_count, GROUP, col_count) - 8) * down_scales[:, None, :]
-    ).astype(jnp.float32) * CODE_STEP
-    down_rows = down_weight.astype(jnp.bfloat16).reshape(group_count * GROUP, col_count)
-    stacked = jnp.concatenate([down_rows, out_weight], axis=0)
+    rotated = blocks_now.reshape(tok_rows, local_blocks * BLOCK)
+
+    own_rows = down_codes.shape[0] // sides
+    scale_rows = jnp.repeat(down_scales, GROUP, axis=0)
+    codes = lax.dynamic_slice_in_dim(down_codes, group_index * own_rows, own_rows, 0)
+    scales = lax.dynamic_slice_in_dim(scale_rows, group_index * own_rows, own_rows, 0)
+    down_rows = (((codes - 8) * scales).astype(jnp.float32) * CODE_STEP).astype(jnp.bfloat16)
+    own_out = out_weight.shape[0] // sides
+    out_rows = lax.dynamic_slice_in_dim(out_weight, group_index * own_out, own_out, 0)
+
+    half = rotated.shape[1] // sides
+    rows = half // CHUNKS
     partials = jnp.dot(
-        joined,
-        lax.all_gather(stacked, "seq", axis=1, tiled=True),
-        preferred_element_type=jnp.float32,
+        attended, gathered(out_rows), preferred_element_type=jnp.float32
     )
+    for chunk in range(CHUNKS):
+        piece = down_rows[chunk * rows : (chunk + 1) * rows]
+        for bit_index in range(tp_count.bit_length() - 1):
+            partner = swapped(piece, "tp", bit_index)
+            high_side = jnp.right_shift(tp_index, bit_index) % 2
+            own_values = piece.astype(jnp.float32)
+            other_values = partner.astype(jnp.float32)
+            piece = jnp.where(
+                high_side == 0, own_values + other_values, other_values - own_values
+            ).astype(jnp.bfloat16)
+        left = jnp.concatenate(
+            [
+                rotated[:, side * half + chunk * rows : side * half + (chunk + 1) * rows]
+                for side in range(sides)
+            ],
+            axis=1,
+        )
+        partials = partials + jnp.dot(left, gathered(piece), preferred_element_type=jnp.float32)
     layer_update = lax.psum_scatter(
         partials.astype(jnp.bfloat16), "tp", scatter_dimension=0, tiled=True
     )

time: 552 us -> 670 us (1.21); the launches traced: 548 us -> 659 us
  local copies, waits for them, and re-layouts: 42 us -> 131 us
  waiting for transfers between devices: 345 us -> 360 us
  matrix products: 85.8 us -> 97.9 us
  other arithmetic: 49.7 us -> 41.3 us
    all_gather x1 -> x8, waiting for transfers between devices: 0.01 us -> 68.8 us  [the longest x4 68.8 us: gathered(): return lax.all_gather(wide, 'seq', axis=1, tiled=True)]
    ppermute x2 -> x6, waiting for transfers between devices: 290 us -> 235 us  [swapped(): lax.ppermute(x, axis, [(i, i ^ 1 << stride) for i in range(lax.axis_size(...]
    unnamed x23 -> x45, local copies, waits for them, and re-layouts: 17 us -> 57.6 us
    slice x0 -> x3, local copies, waits for them, and re-layouts: none -> 18.6 us  [the longest x1 14.2 us: section_pairs(): lower_half = paired[:, :, 1]]
    convert_element_type x1 -> x2, local copies, waits for them, and re-layouts: 11.1 us -> 26.4 us  [section_pairs(): paired = blocks_now.reshape(row_count, block_count >> section_level + 1,...]
    reshape x0 -> x1, local copies, waits for them, and re-layouts: none -> 11.9 us  [per_device(): hidden.reshape(tok_rows * local_blocks, BLOCK)]
    dot_general x3 -> x5, matrix products: 50.3 us -> 60 us  [the longest x3 36.5 us: per_device(): jnp.dot(left, gathered(piece), preferred_element_type=jnp.float32)]
    convert_element_type x3 -> x5, other arithmetic: 26.5 us -> 18.3 us  [the longest x4 12.1 us: per_device(): piece = jnp.where(high_side == 0, own_values + other_values, other_values...]
  transfers between devices with their start and end apart: 6 -> 17, of which waited for: 3 -> 9; matrix products, arithmetic and copies ran while one was open for 24% -> 32% of each run, Pallas kernels for 0% -> 0%
where the time goes in v1:
time: 670 us; the launch traced here: 659 us
  waiting for transfers between devices  360 us (54%)
  local copies, waits for them, and re-layouts  131 us (20%)
  matrix products  97.9 us (15%)
  other arithmetic  41.3 us (6%)
  starting transfers between devices  15 us (2%)
  between operations  14.7 us (2%)
    ppermute x6, waiting for transfers between devices, swapped(): lax.ppermute(x, axis, [(i, i ^ 1 << stride) for i in range(lax.axis_size(...  235 us
    all_gather x4, waiting for transfers between devices, gathered(): return lax.all_gather(wide, 'seq', axis=1, tiled=True)  68.8 us
    unnamed x45, local copies, waits for them, and re-layouts  57.6 us
    reduce_scatter x1, waiting for transfers between devices, per_device(): lax.psum_scatter(partials.astype(jnp.bfloat16), 'tp', scatter_dimension=0...  54.3 us
    dot_general x3, matrix products, per_device(): jnp.dot(left, gathered(piece), preferred_element_type=jnp.float32)  36.5 us
    convert_element_type x2, local copies, waits for them, and re-layouts, section_pairs(): paired = blocks_now.reshape(row_count, block_count >> section_level + 1,...  26.4 us
    dot_general x1, matrix products, per_device(): jnp.dot(hidden.reshape(tok_rows * local_blocks, BLOCK), mixer, preferred_...  14.9 us
    dot_general x1, matrix products, per_device(): jnp.einsum('kgqs,skd->qkgd', weights_soft, value_rows, preferred_element_...  14.6 us
  transfers between devices with their start and end apart: 17, of which 9 were waited for; matrix products, arithmetic and copies ran while one was open for 32% of the time, Pallas kernels for 0%

profile of v1, /device:TPU:0, one launch (start us, length us, event | category | flops | bytes accessed | tf_op | source)
XLA Modules:
  0.0 659.5 jit_solution(1177588082147596731)
XLA Ops:
  7.7 7.9 %broadcast_in_dim.12 = s32[42,128,672]{1,0,2:T(8,128)} broadcast(s32[42,672]{0,1:T(8,128)S(1)} %copy.62), dimensions={0,2} | broadcast | bytes 14563584 | tf_op jit(solution)/shard_map/broadcast_in_dim | solution.py:144
  15.6 17.7 %copy.83 = s32[84,8,42,128]{3,1,2,0:T(8,128)} copy(s32[84,8,42,128]{3,2,1,0:T(8,128)} %bitcast.61) | data formatting | bytes 28901376
  33.3 6.2 multiply_convert_fusion.1
  47.1 25.6 %collective-permute-done.6 = bf16[896,672]{0,1:T(8,128)(2,1)} collective-permute-done((bf16[896,672]{0,1:T(8,128)(2,1)}, bf16[896,672]{0,1:T(8,128)(2,1)}, u32[]{:S(2)}, u32[]{:S(2)}) %collective-permute-start.6) | collective-permute-done | bytes 1204256 | tf_op jit(solution)/shard_map/ppermute | solution.py:27
  72.7 25.8 %collective-permute-done.4 = bf16[896,672]{0,1:T(8,128)(2,1)} collective-permute-done((bf16[896,672]{0,1:T(8,128)(2,1)}, bf16[896,672]{0,1:T(8,128)(2,1)}, u32[]{:S(2)}, u32[]{:S(2)}) %collective-permute-start.4) | collective-permute-done | bytes 1204256 | tf_op jit(solution)/shard_map/ppermute | solution.py:27
  98.5 25.0 %collective-permute-done.2 = bf16[896,672]{0,1:T(8,128)(2,1)} collective-permute-done((bf16[896,672]{0,1:T(8,128)(2,1)S(1)}, bf16[896,672]{0,1:T(8,128)(2,1)}, u32[]{:S(2)}, u32[]{:S(2)}) %collective-permute-start.2) | collective-permute-done | bytes 1204256 | tf_op jit(solution)/shard_map/ppermute | solution.py:27
  123.5 6.0 fusion.20
  133.2 51.0 %collective-permute-done.5 = bf16[896,672]{0,1:T(8,128)(2,1)} collective-permute-done((bf16[896,672]{0,1:T(8,128)(2,1)}, bf16[896,672]{0,1:T(8,128)(2,1)}, u32[]{:S(2)}, u32[]{:S(2)}) %collective-permute-start.5) | collective-permute-done | bytes 1204256 | tf_op jit(solution)/shard_map/ppermute | solution.py:27
  184.2 3.2 fusion.18
  187.7 54.2 %collective-permute-done.3 = bf16[896,672]{0,1:T(8,128)(2,1)S(1)} collective-permute-done((bf16[896,672]{0,1:T(8,128)(2,1)S(1)}, bf16[896,672]{0,1:T(8,128)(2,1)S(1)}, u32[]{:S(2)}, u32[]{:S(2)}) %collective-permute-start.3) | collective-permute-done | bytes 1204256 | tf_op jit(solution)/shard_map/ppermute | solution.py:27
  243.5 53.4 %collective-permute-done.7 = bf16[896,672]{0,1:T(8,128)(2,1)S(1)} collective-permute-done((bf16[896,672]{0,1:T(8,128)(2,1)S(1)}, bf16[896,672]{0,1:T(8,128)(2,1)S(1)}, u32[]{:S(2)}, u32[]{:S(2)}) %collective-permute-start.7) | collective-permute-done | bytes 1204256 | tf_op jit(solution)/shard_map/ppermute | solution.py:27
  308.9 11.9 %reshape.189 = bf16[2048,1344]{1,0:T(8,128)(2,1)} reshape(bf16[512,5376]{1,0:T(8,128)(2,1)} %param.13) | data formatting | bytes 11010048 | tf_op jit(solution)/shard_map/reshape | solution.py:136
  320.9 14.9 %convert_bitcast_fusion = f32[2048,1344]{0,1:T(8,128)} fusion(bf16[1344,1344]{1,0:T(8,128)(2,1)} %constant.83.clone, bf16[2048,1344]{1,0:T(8,128)(2,1)} %reshape.189), kind=kOutput, calls=%fused_computation.10 | convolution fusion | flops 7407009792 | bytes 20127744 | tf_op jit(solution)/shard_map/dot_general | solution.py:135
  335.7 12.2 %copy.59 = f32[2048,1344]{1,0:T(8,128)} copy(f32[2048,1344]{0,1:T(8,128)} %convert_bitcast_fusion) | data formatting | bytes 22020096 | tf_op jit(solution)/shard_map/convert_element_type | solution.py:65
  347.9 14.2 %reshape.193 = f32[512,2,2,1,1344]{4,2,1,0,3:T(2,128)} reshape(f32[2048,1344]{1,0:T(8,128)} %copy.59) | data formatting | bytes 22020096 | tf_op jit(solution)/shard_map/convert_element_type | solution.py:65
  362.6 14.2 %fusion.50 = (f32[512,2,1,1,1344]{4,2,1,0,3:T(1,128)}, f32[512,2,1,1,1344]{4,2,1,0,3:T(1,128)}) fusion(f32[512,2,2,1,1344]{4,2,1,0,3:T(2,128)} %reshape.193), kind=kLoop, calls=%fused_computation.93 | loop fusion | bytes 22020096 | tf_op jit(solution)/shard_map/slice | solution.py:67
  376.8 14.9 %copy.73 = f32[512,2,1,1,1344]{0,4,3,2,1:T(8,128)} copy(f32[512,2,1,1,1344]{4,2,1,0,3:T(1,128)} %get-tuple-element.6) | data formatting | bytes 11010048
  391.7 14.7 %copy.74 = f32[512,2,1,1,1344]{0,4,3,2,1:T(8,128)} copy(f32[512,2,1,1,1344]{4,2,1,0,3:T(1,128)} %get-tuple-element.5) | data formatting | bytes 11010048
  408.9 5.9 fusion.9
  417.3 3.4 add_convert_fusion.1
  426.3 3.5 collective-permute-start.1
  431.5 4.8 copy.51
  446.3 12.8 %fusion.37 = f32[4,1536,512,2]{2,1,3,0:T(8,128)} fusion(bf16[1536,4,128,1]{0,2,3,1:T(8,128)(2,1)S(1)} %bitcast.65, bf16[512,4,2,64]{3,0,2,1:T(8,128)(2,1)S(1)} %bitcast.71, bf16[512,4,2,64]{3,0,2,1:T(8,128)(2,1)S(1)} %bitcast.69), kind=kOutput, calls=%fused_computation.79 | convolution fusion | flops 1612709888 | bytes 27787264 | tf_op jit(solution)/shard_map/qkgd,skd->kgqs/dot_general | solution.py:115
  459.2 10.4 %fusion.56 = f32[4,2,512]{2,1,0:T(2,128)S(1)} fusion(pred[512,1536]{0,1:T(8,128)(4,1)S(1)} %copy-done.18, bf16[1536,4,128,1]{0,2,3,1:T(8,128)(2,1)S(1)} %bitcast.66, bf16[512,4,2,64]{3,0,2,1:T(8,128)(2,1)} %bitcast.72, bf16[512,4,2,64]{3,0,2,1:T(8,128)(2,1)} %bitcast.70), kind=kOutput, calls=%fused_computation.99 | convolution fusion | flops 1637877248 | bytes 3424256 | tf_op jit(solution)/shard_map/sub | solution.py:123
  469.6 14.6 %fusion.36 = bf16[4,128,2,512]{3,1,2,0:T(8,128)(2,1)} fusion(bf16[1536,4,128,1]{0,2,3,1:T(8,128)(2,1)} %bitcast.74, f32[4,2,512]{2,1,0:T(2,128)S(1)} %fusion.56, f32[4,1536,512,2]{2,1,3,0:T(8,128)} %fusion.37, pred[512,1536]{0,1:T(8,128)(4,1)S(1)} %copy-done.18), kind=kOutput, calls=%fused_computation.70 | convolution fusion | flops 1642599936 | bytes 28590080 | tf_op jit(solution)/shard_map/kgqs,skd->qkgd/dot_general | solution.py:127
  484.2 8.6 %fusion.57 = f32[512,2688]{1,0:T(8,128)} fusion(bf16[512,1024]{0,1:T(8,128)(2,1)} %bitcast.75, bf16[1024,2688]{0,1:T(8,128)(2,1)} %all-gather.11.cloned.1.call-done), kind=kOutput, calls=%fused_computation.100 | convolution fusion | flops 2818572288 | bytes 12058624 | tf_op jit(solution)/shard_map/dot_general | solution.py:153
  492.8 11.2 %fusion.29 = f32[512,2688]{1,0:T(8,128)} fusion(bf16[1792,2688]{0,1:T(8,128)(2,1)} %all-gather.19.cloned.1.call-done, bf16[512,896]{0,1:T(8,128)(2,1)S(1)} %copy-done.16, bf16[512,896]{0,1:T(8,128)(2,1)S(1)} %copy-done.17), kind=kOutput, calls=%fused_computation.63 | convolution fusion | flops 4936171520 | bytes 16973824 | tf_op jit(solution)/shard_map/dot_general | solution.py:173
  504.0 13.0 %all-gather.15.cloned.1.call-done = bf16[1792,2688]{0,1:T(8,128)(2,1)} async-done(((bf16[1792,672]{0,1:T(8,128)(2,1)}), bf16[1792,2688]{0,1:T(8,128)(2,1)}) %all-gather.15.cloned.1.call-update) | async-done | bytes 9633808 | tf_op jit(solution)/shard_map/all_gather | solution.py:45
  517.0 11.2 %fusion.25 = f32[512,2688]{1,0:T(8,128)} fusion(bf16[1792,2688]{0,1:T(8,128)(2,1)} %all-gather.15.cloned.1.call-done, bf16[512,896]{0,1:T(8,128)(2,1)S(1)} %copy-done.15, bf16[512,896]{0,1:T(8,128)(2,1)} %get-tuple-element.16), kind=kOutput, calls=%fused_computation.59 | convolution fusion | flops 4936171520 | bytes 16973824 | tf_op jit(solution)/shard_map/dot_general | solution.py:173
  528.3 55.7 %all-gather.23.cloned.1.call-done = bf16[1792,2688]{0,1:T(8,128)(2,1)} async-done(((bf16[1792,672]{0,1:T(8,128)(2,1)}), bf16[1792,2688]{0,1:T(8,128)(2,1)}) %all-gather.23.cloned.1.call-update) | async-done | bytes 9633808 | tf_op jit(solution)/shard_map/all_gather | solution.py:45
  584.0 14.2 %add_convert_fusion = bf16[512,2688]{1,0:T(8,128)(2,1)} fusion(f32[512,2688]{1,0:T(8,128)} %fusion.29, f32[512,2688]{1,0:T(8,128)} %fusion.57, f32[512,2688]{1,0:T(8,128)} %fusion.25, bf16[1792,2688]{0,1:T(8,128)(2,1)} %all-gather.23.cloned.1.call-done, bf16[512,896]{0,1:T(8,128)(2,1)S(1)} %copy-done.14, bf16[512,896]{0,1:T(8,128)(2,1)S(1)} %copy-done.13), kind=kOutput, calls=%fused_computation.15 | convolution fusion | flops 4941676544 | bytes 30736384 | tf_op jit(solution)/shard_map/dot_general | solution.py:173
  598.2 54.3 %reduce-scatter.2.cloned.1.call-done = bf16[128,2688]{1,0:T(8,128)(2,1)} async-done(((bf16[512,2688]{1,0:T(8,128)(2,1)}), bf16[128,2688]{1,0:T(8,128)(2,1)}) %reduce-scatter.2.cloned.1.call-update) | async-done | bytes 688144 | tf_op jit(solution)/shard_map/reduce_scatter | solution.py:174
  (101 shorter events, 48.5 us)
Async XLA Ops:
  6.5 125.7 %copy-start = (bf16[1024,672]{0,1:T(8,128)(2,1)S(1)}, bf16[1024,672]{0,1:T(8,128)(2,1)}, u32[]{:S(2)}) copy-start(bf16[1024,672]{0,1:T(8,128)(2,1)} %param.16) | copy-start | bytes 4128772
  6.5 292.0 %all-gather.9.cloned.1.call-start = ((), (), s32[]{:S(2)}) async-start(), calls=%async_computation.1 | async-start | bytes 2064384 | tf_op jit(solution)/shard_map/all_gather | solution.py:44
  39.5 2.6 copy-start.2
  42.1 30.7 %collective-permute-start.6 = (bf16[896,672]{0,1:T(8,128)(2,1)}, bf16[896,672]{0,1:T(8,128)(2,1)}, u32[]{:S(2)}, u32[]{:S(2)}) collective-permute-start(bf16[896,672]{0,1:T(8,128)(2,1)} %get-tuple-element.22), channel_id=1, source_target_pairs={{0,1},{1,0},{2,3},{3,2},{4,5},{5,4},{6,7},{7,6},{8,9},{9,8},{10,11... | collective-permute-start | bytes 3612680 | tf_op jit(solution)/shard_map/ppermute | solution.py:27
  45.1 53.4 %collective-permute-start.4 = (bf16[896,672]{0,1:T(8,128)(2,1)}, bf16[896,672]{0,1:T(8,128)(2,1)}, u32[]{:S(2)}, u32[]{:S(2)}) collective-permute-start(bf16[896,672]{0,1:T(8,128)(2,1)} %get-tuple-element.23), channel_id=1, source_target_pairs={{0,1},{1,0},{2,3},{3,2},{4,5},{5,4},{6,7},{7,6},{8,9},{9,8},{10,11... | collective-permute-start | bytes 3612680 | tf_op jit(solution)/shard_map/ppermute | solution.py:27
  45.1 78.4 %collective-permute-start.2 = (bf16[896,672]{0,1:T(8,128)(2,1)S(1)}, bf16[896,672]{0,1:T(8,128)(2,1)}, u32[]{:S(2)}, u32[]{:S(2)}) collective-permute-start(bf16[896,672]{0,1:T(8,128)(2,1)S(1)} %get-tuple-element.24), channel_id=1, source_target_pairs={{0,1},{1,0},{2,3},{3,2},{4,5},{5,4},{6,7},{7,6},{8,9},{9,8},{10,11... | collective-permute-start | bytes 3612680 | tf_op jit(solution)/shard_map/ppermute | solution.py:27
  129.5 54.7 %collective-permute-start.5 = (bf16[896,672]{0,1:T(8,128)(2,1)}, bf16[896,672]{0,1:T(8,128)(2,1)}, u32[]{:S(2)}, u32[]{:S(2)}) collective-permute-start(bf16[896,672]{0,1:T(8,128)(2,1)} %get-tuple-element.20), channel_id=1, source_target_pairs={{0,2},{1,3},{2,0},{3,1},{4,6},{5,7},{6,4},{7,5},{8,10},{9,11},{10,... | collective-permute-start | bytes 3612680 | tf_op jit(solution)/shard_map/ppermute | solution.py:27
  133.1 54.5 %copy-start.7 = (bf16[896,672]{0,1:T(8,128)(2,1)S(1)}, bf16[896,672]{0,1:T(8,128)(2,1)}, u32[]{:S(2)}) copy-start(bf16[896,672]{0,1:T(8,128)(2,1)} %get-tuple-element.21) | copy-start | bytes 3612676
  133.1 166.0 %all-gather.17.cloned.1.call-start = ((), (), s32[]{:S(2)}) async-start(), calls=%async_computation.5 | async-start | bytes 3612672 | tf_op jit(solution)/shard_map/all_gather | solution.py:44
  187.3 112.3 %all-gather.13.cloned.1.call-start = ((), (), s32[]{:S(2)}) async-start(), calls=%async_computation.3 | async-start | bytes 3612672 | tf_op jit(solution)/shard_map/all_gather | solution.py:44
  187.6 54.3 %collective-permute-start.3 = (bf16[896,672]{0,1:T(8,128)(2,1)S(1)}, bf16[896,672]{0,1:T(8,128)(2,1)S(1)}, u32[]{:S(2)}, u32[]{:S(2)}) collective-permute-start(bf16[896,672]{0,1:T(8,128)(2,1)S(1)} %copy-done.7), channel_id=1, source_target_pairs={{0,2},{1,3},{2,0},{3,1},{4,6},{5,7},{6,4},{7,5},{8,10},{9,11},{10,... | collective-permute-start | bytes 3612680 | tf_op jit(solution)/shard_map/ppermute | solution.py:27
  243.4 118.7 %all-gather.21.cloned.1.call-start = ((), (), s32[]{:S(2)}) async-start(), calls=%async_computation.7 | async-start | bytes 3612672 | tf_op jit(solution)/shard_map/all_gather | solution.py:44
  243.4 53.5 %collective-permute-start.7 = (bf16[896,672]{0,1:T(8,128)(2,1)S(1)}, bf16[896,672]{0,1:T(8,128)(2,1)S(1)}, u32[]{:S(2)}, u32[]{:S(2)}) collective-permute-start(bf16[896,672]{0,1:T(8,128)(2,1)S(1)} %get-tuple-element.19), channel_id=1, source_target_pairs={{0,2},{1,3},{2,0},{3,1},{4,6},{5,7},{6,4},{7,5},{8,10},{9,11},{10,... | collective-permute-start | bytes 3612680 | tf_op jit(solution)/shard_map/ppermute | solution.py:27
  298.4 185.7 %all-gather.11.cloned.1.call-start = ((), (), s32[]{:S(2)}) async-start(), calls=%async_computation.2 | async-start | bytes 6881280 | tf_op jit(solution)/shard_map/all_gather | solution.py:45
  299.0 193.8 %all-gather.19.cloned.1.call-start = ((), (), s32[]{:S(2)}) async-start(), calls=%async_computation.6 | async-start | bytes 12042240 | tf_op jit(solution)/shard_map/all_gather | solution.py:45
  299.6 217.4 %all-gather.15.cloned.1.call-start = ((), (), s32[]{:S(2)}) async-start(), calls=%async_computation.4 | async-start | bytes 12042240 | tf_op jit(solution)/shard_map/all_gather | solution.py:45
  300.4 283.6 %all-gather.23.cloned.1.call-start = ((), (), s32[]{:S(2)}) async-start(), calls=%async_computation.8 | async-start | bytes 12042240 | tf_op jit(solution)/shard_map/all_gather | solution.py:45
  306.3 120.0 %collective-permute-start = (bf16[512,2,512]{0,2,1:T(8,128)(2,1)}, bf16[512,2,512]{0,2,1:T(8,128)(2,1)}, u32[]{:S(2)}, u32[]{:S(2)}) collective-permute-start(bf16[512,2,512]{0,2,1:T(8,128)(2,1)} %pad_maximum_fusion.1), channel_id=1, source_target_pairs={{0,4},{4,8},{8,12},{1,5},{5,9},{9,13},{2,6},{6,10},{10,14},{3,7},{... | collective-permute-start | bytes 3145736 | tf_op jit(solution)/shard_map/ppermute | solution.py:23
  362.1 290.4 %reduce-scatter.2.cloned.1.call-start = ((), (), s32[]{:S(2)}) async-start(), calls=%async_computation.9 | async-start | bytes 3440640 | tf_op jit(solution)/shard_map/reduce_scatter | solution.py:174
  391.7 14.7 %copy-start.11 = (bf16[512,1024]{1,0:T(8,128)(2,1)S(1)}, bf16[512,1024]{1,0:T(8,128)(2,1)}, u32[]{:S(2)}) copy-start(bf16[512,1024]{1,0:T(8,128)(2,1)} %param.9) | copy-start | bytes 3145732
  420.7 2.6 copy-start.4
  426.3 15.6 %collective-permute-start.1 = (bf16[512,2,512]{0,2,1:T(8,128)(2,1)}, bf16[512,2,512]{0,2,1:T(8,128)(2,1)}, u32[]{:S(2)}, u32[]{:S(2)}) collective-permute-start(bf16[512,2,512]{0,2,1:T(8,128)(2,1)} %collective-permute-done), channel_id=1, source_target_pairs={{0,4},{4,8},{8,12},{1,5},{5,9},{9,13},{2,6},{6,10},{10,14},{3,7},{... | collective-permute-start | bytes 3145736 | tf_op jit(solution)/shard_map/ppermute | solution.py:23
  431.5 6.9 %copy-start.12 = (f32[512,64]{1,0:T(8,128)S(1)}, f32[512,64]{1,0:T(8,128)}, u32[]{:S(2)}) copy-start(f32[512,64]{1,0:T(8,128)} %copy.56) | copy-start | bytes 393220
  440.3 6.1 copy-start.8
  440.3 6.0 copy-start.9
  446.3 12.8 %copy-start.18 = (pred[512,1536]{0,1:T(8,128)(4,1)S(1)}, pred[512,1536]{0,1:T(8,128)(4,1)}, u32[]{:S(2)}) copy-start(pred[512,1536]{0,1:T(8,128)(4,1)} %fusion.8) | copy-start | bytes 2359300
  484.2 8.6 %copy-start.16 = (bf16[512,896]{0,1:T(8,128)(2,1)S(1)}, bf16[512,896]{0,1:T(8,128)(2,1)}, u32[]{:S(2)}) copy-start(bf16[512,896]{0,1:T(8,128)(2,1)} %get-tuple-element.13) | copy-start | bytes 2752516
  484.2 8.6 %copy-start.17 = (bf16[512,896]{0,1:T(8,128)(2,1)S(1)}, bf16[512,896]{0,1:T(8,128)(2,1)}, u32[]{:S(2)}) copy-start(bf16[512,896]{0,1:T(8,128)(2,1)} %get-tuple-element.14) | copy-start | bytes 2752516
  492.8 24.2 %copy-start.15 = (bf16[512,896]{0,1:T(8,128)(2,1)S(1)}, bf16[512,896]{0,1:T(8,128)(2,1)}, u32[]{:S(2)}) copy-start(bf16[512,896]{0,1:T(8,128)(2,1)} %get-tuple-element.15) | copy-start | bytes 2752516
  517.0 67.0 %copy-start.13 = (bf16[512,896]{0,1:T(8,128)(2,1)S(1)}, bf16[512,896]{0,1:T(8,128)(2,1)}, u32[]{:S(2)}) copy-start(bf16[512,896]{0,1:T(8,128)(2,1)} %get-tuple-element.11) | copy-start | bytes 2752516
  517.0 67.0 %copy-start.14 = (bf16[512,896]{0,1:T(8,128)(2,1)S(1)}, bf16[512,896]{0,1:T(8,128)(2,1)}, u32[]{:S(2)}) copy-start(bf16[512,896]{0,1:T(8,128)(2,1)} %get-tuple-element.12) | copy-start | bytes 2752516
  584.0 68.5 %copy-start.1 = (bf16[1024,672]{0,1:T(8,128)(2,1)S(1)}, bf16[1024,672]{0,1:T(8,128)(2,1)}, u32[]{:S(2)}) copy-start(bf16[1024,672]{0,1:T(8,128)(2,1)} %param.16) | copy-start | bytes 4128772
  (4 other events, 8.4 us)
Sparse Core Ops, SparseCore 0:
  133.3 24.2 all-gather.8
  187.5 37.6 all-gather.16
  243.5 35.1 all-gather.12
  298.6 34.8 all-gather.20
  334.9 41.9 all-gather.10
  378.2 66.7 all-gather.18
  446.6 70.4 all-gather.14
  518.6 65.3 all-gather.22
  598.3 54.1 reduce-scatter.1

commit v2 on v1

--- a/solution.py
+++ b/solution.py
@@ -7,8 +7,6 @@
 HD = 128
 WINDOW = 1024
 GROUP = 128
-BLOCK = 1344
-CHUNKS = 3
 
 
 ROPE_BASE = 10000.0
@@ -37,12 +35,27 @@
     places = np.arange(order)
     paley[1:, 1:] += legendre[(places[None, :] - places[:, None]) % order]
     pair = np.array([[1, 1], [1, -1]])
-    return jnp.asarray(np.kron(np.kron(np.kron(pair, pair), pair), paley), jnp.bfloat16)
+    return jnp.asarray(
+        np.kron(np.kron(np.kron(np.kron(pair, pair), pair), pair), paley), jnp.bfloat16
+    )
 
 
 def gathered(piece):
-    wide = lax.all_gather(piece, "group", axis=0, tiled=True)
-    return lax.all_gather(wide, "seq", axis=1, tiled=True)
+    held = {0: jnp.concatenate([piece, swapped(piece, "group", 0)], axis=0)}
+    for bit_index in reversed(range(lax.axis_size("seq").bit_length() - 1)):
+        for distance, columns in list(held.items()):
+            held[distance | 1 << bit_index] = swapped(columns, "seq", bit_index)
+    return held
+
+
+def own_and_other(rows, group_index, begin, count, half):
+    return jnp.concatenate(
+        [
+            lax.dynamic_slice_in_dim(rows, side * half + begin, count, 1)
+            for side in (group_index, 1 - group_index)
+        ],
+        axis=1,
+    )
 
 
 def rotary(values, cosine, sine_part):
@@ -56,17 +69,6 @@
         ],
         axis=-1,
     )
-
-
-def section_pairs(blocks_now, section_level):
-    row_count, block_count, width_cols = blocks_now.shape
-    paired = blocks_now.reshape(
-        row_count, block_count >> section_level + 1, 2, 1 << section_level, width_cols
-    ).astype(jnp.float32)
-    upper_half = paired[:, :, 0]
-    lower_half = paired[:, :, 1]
-    mixed = jnp.stack([upper_half + lower_half, upper_half - lower_half], axis=2)
-    return mixed.astype(jnp.bfloat16).reshape(row_count, block_count, width_cols)
 
 
 def per_device(
@@ -128,53 +130,62 @@
         "kgqs,skd->qkgd", weights_soft, value_rows, preferred_element_type=jnp.float32
     )
     attended = attended.astype(jnp.bfloat16).reshape(tok_rows, heads_dev * HD)
+    group_index = lax.axis_index("group")
     mixer = block_mixer()
-    local_blocks = hidden.shape[1] // BLOCK
-    group_index = lax.axis_index("group")
-    sides = lax.axis_size("group")
-    mixed = jnp.dot(
-        hidden.reshape(tok_rows * local_blocks, BLOCK), mixer, preferred_element_type=jnp.float32
-    )
-    blocks_now = (mixed * INV_ROOT).astype(jnp.bfloat16).reshape(tok_rows, local_blocks, BLOCK)
-    for section_level in range(local_blocks.bit_length() - 1):
-        blocks_now = section_pairs(blocks_now, section_level)
-    rotated = blocks_now.reshape(tok_rows, local_blocks * BLOCK)
-
-    own_rows = down_codes.shape[0] // sides
+    width = mixer.shape[0]
+    mixed = [
+        jnp.dot(hidden[:, first : first + width], mixer, preferred_element_type=jnp.float32)
+        for first in range(0, hidden.shape[1], width)
+    ]
+    stride = 1
+    while stride < len(mixed):
+        mixed = [
+            mixed[i] + mixed[i ^ stride] if i & stride == 0 else mixed[i ^ stride] - mixed[i]
+            for i in range(len(mixed))
+        ]
+        stride *= 2
+    rotated = jnp.concatenate([(part * INV_ROOT).astype(jnp.bfloat16) for part in mixed], axis=1)
+
+    half = rotated.shape[1] // 2
+    out_half = out_weight.shape[0] // 2
     scale_rows = jnp.repeat(down_scales, GROUP, axis=0)
-    codes = lax.dynamic_slice_in_dim(down_codes, group_index * own_rows, own_rows, 0)
-    scales = lax.dynamic_slice_in_dim(scale_rows, group_index * own_rows, own_rows, 0)
-    down_rows = (((codes - 8) * scales).astype(jnp.float32) * CODE_STEP).astype(jnp.bfloat16)
-    own_out = out_weight.shape[0] // sides
-    out_rows = lax.dynamic_slice_in_dim(out_weight, group_index * own_out, own_out, 0)
-
-    half = rotated.shape[1] // sides
-    rows = half // CHUNKS
-    partials = jnp.dot(
-        attended, gathered(out_rows), preferred_element_type=jnp.float32
-    )
-    for chunk in range(CHUNKS):
-        piece = down_rows[chunk * rows : (chunk + 1) * rows]
+    unit = half // 21
+    out_piece = lax.dynamic_slice_in_dim(out_weight, group_index * out_half, out_half, 0)
+    tokens_left = own_and_other(attended, group_index, 0, out_half, out_half)
+    totals = {
+        distance: jnp.dot(tokens_left, columns, preferred_element_type=jnp.float32)
+        for distance, columns in gathered(out_piece).items()
+    }
+    tied = None
+    for first, last in ((0, 6), (6, 11), (11, 16), (16, 21)):
+        begin, rows = first * unit, (last - first) * unit
+        codes = lax.dynamic_slice_in_dim(down_codes, group_index * half + begin, rows, 0)
+        scales = lax.dynamic_slice_in_dim(scale_rows, group_index * half + begin, rows, 0)
+        piece = (((codes - 8) * scales).astype(jnp.float32) * CODE_STEP).astype(jnp.bfloat16)
         for bit_index in range(tp_count.bit_length() - 1):
+            if bit_index == 0 and tied is not None:
+                piece, tied = lax.optimization_barrier((piece, tied))
             partner = swapped(piece, "tp", bit_index)
+            if bit_index == 0:
+                tied = partner
             high_side = jnp.right_shift(tp_index, bit_index) % 2
             own_values = piece.astype(jnp.float32)
             other_values = partner.astype(jnp.float32)
             piece = jnp.where(
                 high_side == 0, own_values + other_values, other_values - own_values
             ).astype(jnp.bfloat16)
-        left = jnp.concatenate(
-            [
-                rotated[:, side * half + chunk * rows : side * half + (chunk + 1) * rows]
-                for side in range(sides)
-            ],
-            axis=1,
-        )
-        partials = partials + jnp.dot(left, gathered(piece), preferred_element_type=jnp.float32)
-    layer_update = lax.psum_scatter(
-        partials.astype(jnp.bfloat16), "tp", scatter_dimension=0, tiled=True
-    )
-    return layer_update
+        left = own_and_other(rotated, group_index, begin, rows, half)
+        for distance, columns in gathered(piece).items():
+            totals[distance] += jnp.dot(left, columns, preferred_element_type=jnp.float32)
+    stacked = jnp.stack([totals[d].astype(jnp.bfloat16) for d in sorted(totals)])
+    partials = jnp.concatenate(
+        [
+            lax.dynamic_index_in_dim(stacked, jnp.bitwise_xor(seq_index, s), 0, keepdims=False)
+            for s in range(len(totals))
+        ],
+        axis=1,
+    )
+    return lax.psum_scatter(partials, "tp", scatter_dimension=0, tiled=True)
 
 
 def solution(mesh):

time: 670 us -> 521 us (0.78)
  waiting for transfers between devices: 360 us -> 272 us
  local copies, waits for them, and re-layouts: 131 us -> 52.6 us
  starting transfers between devices: 15 us -> 31.8 us
  other arithmetic: 41.3 us -> 52 us
  matrix products: 97.9 us -> 88.9 us
    all_gather x8 -> x0, waiting for transfers between devices: 68.8 us -> none  [the longest x4 68.8 us: gathered(): return lax.all_gather(wide, 'seq', axis=1, tiled=True)]
    convert_element_type x2 -> x0, local copies, waits for them, and re-layouts: 26.4 us -> none  [section_pairs(): paired = blocks_now.reshape(row_count, block_count >> section_level + 1,...]
    unnamed x45 -> x60, local copies, waits for them, and re-layouts: 57.6 us -> 35.3 us
    slice x3 -> x0, local copies, waits for them, and re-layouts: 18.6 us -> none  [the longest x1 14.2 us: section_pairs(): lower_half = paired[:, :, 1]]
    ppermute x6 -> x28, starting transfers between devices: 7.95 us -> 26 us  [swapped(): lax.ppermute(x, axis, [(i, i ^ 1 << stride) for i in range(lax.axis_size(...]
    concatenate x0 -> x8, other arithmetic: none -> 17.1 us  [the longest x2 10.8 us: per_device(): jnp.concatenate([(part * INV_ROOT).astype(jnp.bfloat16) for part in mixed...]
    ppermute x6 -> x28, waiting for transfers between devices: 235 us -> 219 us  [swapped(): lax.ppermute(x, axis, [(i, i ^ 1 << stride) for i in range(lax.axis_size(...]
    reshape x1 -> x0, local copies, waits for them, and re-layouts: 11.9 us -> none  [per_device(): hidden.reshape(tok_rows * local_blocks, BLOCK)]
  transfers between devices with their start and end apart: 17 -> 31, of which waited for: 9 -> 11; matrix products, arithmetic and copies ran while one was open for 32% -> 30% of each run, Pallas kernels for 0% -> 0%
where the time goes in v2:
time: 521 us; the launch traced here: 513 us
  waiting for transfers between devices  272 us (52%)
  matrix products  88.9 us (17%)
  local copies, waits for them, and re-layouts  52.6 us (10%)
  other arithmetic  52 us (10%)
  starting transfers between devices  31.8 us (6%)
  between operations  15.2 us (3%)
    ppermute x28, waiting for transfers between devices, swapped(): lax.ppermute(x, axis, [(i, i ^ 1 << stride) for i in range(lax.axis_size(...  219 us
    reduce_scatter x1, waiting for transfers between devices, per_device(): return lax.psum_scatter(partials, 'tp', scatter_dimension=0, tiled=True)  52.7 us
    unnamed x60, local copies, waits for them, and re-layouts  35.3 us
    ppermute x28, starting transfers between devices, swapped(): lax.ppermute(x, axis, [(i, i ^ 1 << stride) for i in range(lax.axis_size(...  26 us
    dot_general x2, matrix products, per_device(): jnp.dot(hidden[:, first:first + width], mixer, preferred_element_type=jnp...  26 us
    dot_general x16, matrix products, per_device(): jnp.dot(left, columns, preferred_element_type=jnp.float32)  19.3 us
    dot_general x1, matrix products, per_device(): jnp.einsum('kgqs,skd->qkgd', weights_soft, value_rows, preferred_element_...  13.9 us
    dot_general x1, matrix products, per_device(): jnp.einsum('qkgd,skd->kgqs', grouped, key_rows, preferred_element_type=jn...  13.2 us
  transfers between devices with their start and end apart: 31, of which 11 were waited for; matrix products, arithmetic and copies ran while one was open for 30% of the time, Pallas kernels for 0%

profile of v2, /device:TPU:0, one launch (start us, length us, event | category | flops | bytes accessed | tf_op | source)
XLA Modules:
  0.0 512.5 jit_solution(15400570881000754555)
XLA Ops:
  7.7 7.9 %broadcast_in_dim.12 = s32[42,128,672]{1,0,2:T(8,128)} broadcast(s32[42,672]{0,1:T(8,128)S(1)} %copy.51), dimensions={0,2} | broadcast | bytes 14563584 | tf_op jit(solution)/shard_map/broadcast_in_dim | solution.py:151
  15.6 17.7 %copy.73 = s32[84,8,42,128]{3,1,2,0:T(8,128)} copy(s32[84,8,42,128]{3,2,1,0:T(8,128)} %bitcast.85) | data formatting | bytes 28901376
  33.3 3.6 multiply_convert_fusion.2
  36.8 3.0 collective-permute-start.3
  51.0 2.7 collective-permute-start
  56.2 11.8 %fusion.11 = f32[2688,512]{1,0:T(8,128)S(1)} fusion(bf16[2688,2688]{1,0:T(8,128)(2,1)} %constant.118.clone, bf16[512,5376]{1,0:T(8,128)(2,1)} %param.13), kind=kOutput, calls=%fused_computation.40 | convolution fusion | flops 7398752256 | bytes 22708224 | tf_op jit(solution)/shard_map/dot_general | solution.py:137
  68.1 14.2 %fusion.10 = (bf16[512,2688]{0,1:T(8,128)(2,1)}, bf16[512,2688]{0,1:T(8,128)(2,1)}) fusion(f32[2688,512]{1,0:T(8,128)S(1)} %fusion.11, bf16[2688,2688]{1,0:T(8,128)(2,1)} %constant.118.clone, bf16[512,5376]{1,0:T(8,128)(2,1)S(1)} %bitcast.101), kind=kOutput, calls=%fused_computation.37 | convolution fusion | flops 7407009792 | bytes 28213248 | tf_op jit(solution)/shard_map/dot_general | solution.py:137
  87.4 6.0 %multiply_convert_fusion.3 = (bf16[640,672]{0,1:T(8,128)(2,1)}, bf16[640,672]{0,1:T(8,128)(2,1)}, bf16[640,672]{0,1:T(8,128)(2,1)}) fusion(s32[5376,672]{0,1:T(8,128)} %bitcast.87, s32[]{:T(128)S(6)} %select_n.157, s32[5376,672]{0,1:T(8,128)} %param.14, s32[]{:T(128)S(6)} %select_n.153, s32[]{:T(128)S(6)} %select_n.147), kind=kLoop, calls=%fused_computation.86 | loop fusion | flops 6451200 | bytes 12902412 | tf_op jit(solution)/shard_map/convert_element_type | solution.py:164
  100.8 6.5 %copy.43 = bf16[1024,2,512]{0,2,1:T(8,128)(2,1)} copy(bf16[1024,2,512]{2,1,0:T(2,128)(2,1)} %param.11) | data formatting | bytes 4194304 | tf_op args[2]
  107.4 3.5 fusion.16
  110.9 3.1 collective-permute-start.1
  114.0 4.2 fusion.38
  118.2 6.6 %fusion.49 = (bf16[512,640]{0,1:T(8,128)(2,1)}, bf16[512,640]{0,1:T(8,128)(2,1)}, bf16[512,640]{0,1:T(8,128)(2,1)}, bf16[512,640]{0,1:T(8,128)(2,1)}, bf16[512,640]{0,1:T(8,128)(2,1)}, /*index=5*/bf16[512,640]{0,1:T(8,128)(2,1)}) fusion(s32[]{:T(128)S(6)} %select_n.157, bf16[512,2688]{0,1:T(8,128)(2,1)} %get-tuple-element.15, ...), kind=kLoop, calls=%fused_computation.125 | loop fusion | flops 7864320 | bytes 9437208 | tf_op jit(solution)/shard_map/concatenate | solution.py:147
  127.4 5.8 %collective-permute-done.6 = bf16[640,672]{0,1:T(8,128)(2,1)} collective-permute-done((bf16[640,672]{0,1:T(8,128)(2,1)}, bf16[640,672]{0,1:T(8,128)(2,1)}, u32[]{:S(2)}, u32[]{:S(2)}) %collective-permute-start.6) | collective-permute-done | bytes 860192 | tf_op jit(solution)/shard_map/ppermute | solution.py:25
  135.8 9.2 %collective-permute-done.4 = bf16[768,672]{0,1:T(8,128)(2,1)} collective-permute-done((bf16[768,672]{0,1:T(8,128)(2,1)S(1)}, bf16[768,672]{0,1:T(8,128)(2,1)}, u32[]{:S(2)}, u32[]{:S(2)}) %collective-permute-start.4) | collective-permute-done | bytes 1032224 | tf_op jit(solution)/shard_map/ppermute | solution.py:25
  148.2 2.7 fusion.15
  152.6 10.2 %fusion.79 = f32[4,2,512]{2,1,0:T(2,128)S(1)} fusion(pred[512,1536]{0,1:T(8,128)(4,1)} %fusion.8, bf16[1536,4,128,1]{0,2,3,1:T(8,128)(2,1)S(1)} %bitcast.89, bf16[512,4,2,64]{3,0,2,1:T(8,128)(2,1)} %bitcast.95, bf16[512,4,2,64]{3,0,2,1:T(8,128)(2,1)S(1)} %bitcast.93), kind=kOutput, calls=%fused_computation.164 | convolution fusion | flops 1637877248 | bytes 3424256 | tf_op jit(solution)/shard_map/sub | solution.py:125
  162.8 13.2 %fusion.50 = f32[4,1536,512,2]{2,1,3,0:T(8,128)} fusion(bf16[1536,4,128,1]{0,2,3,1:T(8,128)(2,1)S(1)} %bitcast.90, bf16[512,4,2,64]{3,0,2,1:T(8,128)(2,1)} %bitcast.96, bf16[512,4,2,64]{3,0,2,1:T(8,128)(2,1)S(1)} %bitcast.94), kind=kOutput, calls=%fused_computation.132 | convolution fusion | flops 1612709888 | bytes 27787264 | tf_op jit(solution)/shard_map/qkgd,skd->kgqs/dot_general | solution.py:117
  176.0 13.9 %fusion.33 = bf16[4,128,2,512]{3,1,2,0:T(8,128)(2,1)S(1)} fusion(bf16[1536,4,128,1]{0,2,3,1:T(8,128)(2,1)} %bitcast.98, f32[4,2,512]{2,1,0:T(2,128)S(1)} %fusion.79, f32[4,1536,512,2]{2,1,3,0:T(8,128)} %fusion.50, pred[512,1536]{0,1:T(8,128)(4,1)} %fusion.8), kind=kOutput, calls=%fused_computation.90 | convolution fusion | flops 1642599936 | bytes 28590080 | tf_op jit(solution)/shard_map/kgqs,skd->qkgd/dot_general | solution.py:129
  193.2 3.6 collective-permute-start.10
  201.8 25.8 %collective-permute-done.12 = bf16[640,672]{0,1:T(8,128)(2,1)S(1)} collective-permute-done((bf16[640,672]{0,1:T(8,128)(2,1)S(1)}, bf16[640,672]{0,1:T(8,128)(2,1)S(1)}, u32[]{:S(2)}, u32[]{:S(2)}) %collective-permute-start.12) | collective-permute-done | bytes 860192 | tf_op jit(solution)/shard_map/ppermute | solution.py:25
  228.1 2.8 fusion.72
  230.8 22.9 %collective-permute-done.10 = bf16[640,672]{0,1:T(8,128)(2,1)S(1)} collective-permute-done((bf16[640,672]{0,1:T(8,128)(2,1)S(1)}, bf16[640,672]{0,1:T(8,128)(2,1)S(1)}, u32[]{:S(2)}, u32[]{:S(2)}) %collective-permute-start.10) | collective-permute-done | bytes 860192 | tf_op jit(solution)/shard_map/ppermute | solution.py:25
  258.8 11.7 %collective-permute-done.13 = bf16[640,672]{0,1:T(8,128)(2,1)S(1)} collective-permute-done((bf16[640,672]{0,1:T(8,128)(2,1)S(1)}, bf16[640,672]{0,1:T(8,128)(2,1)S(1)}, u32[]{:S(2)}, u32[]{:S(2)}) %collective-permute-start.13) | collective-permute-done | bytes 860192 | tf_op jit(solution)/shard_map/ppermute | solution.py:25
  272.3 6.1 %collective-permute-start.22 = (bf16[1280,672]{0,1:T(8,128)(2,1)S(1)}, bf16[1280,672]{0,1:T(8,128)(2,1)S(1)}, u32[]{:S(2)}, u32[]{:S(2)}) collective-permute-start(bf16[1280,672]{0,1:T(8,128)(2,1)S(1)} %pad_maximum_fusion.3), channel_id=1, source_target_pairs={{0,8},{4,12},{8,0},{12,4},{1,9},{5,13},{9,1},{13,5},{2,10},{6,14},... | collective-permute-start | bytes 5160968 | tf_op jit(solution)/shard_map/ppermute | solution.py:25
  280.7 20.9 %collective-permute-done.21 = bf16[1536,672]{0,1:T(8,128)(2,1)S(1)} collective-permute-done((bf16[1536,672]{0,1:T(8,128)(2,1)S(1)}, bf16[1536,672]{0,1:T(8,128)(2,1)S(1)}, u32[]{:S(2)}, u32[]{:S(2)}) %collective-permute-start.21) | collective-permute-done | bytes 2064416 | tf_op jit(solution)/shard_map/ppermute | solution.py:25
  307.3 31.2 %collective-permute-done.22 = bf16[1280,672]{0,1:T(8,128)(2,1)S(1)} collective-permute-done((bf16[1280,672]{0,1:T(8,128)(2,1)S(1)}, bf16[1280,672]{0,1:T(8,128)(2,1)S(1)}, u32[]{:S(2)}, u32[]{:S(2)}) %collective-permute-start.22) | collective-permute-done | bytes 1720352 | tf_op jit(solution)/shard_map/ppermute | solution.py:25
  340.7 27.2 %collective-permute-done.20 = bf16[1024,672]{0,1:T(8,128)(2,1)S(1)} collective-permute-done((bf16[1024,672]{0,1:T(8,128)(2,1)}, bf16[1024,672]{0,1:T(8,128)(2,1)S(1)}, u32[]{:S(2)}, u32[]{:S(2)}) %collective-permute-start.20) | collective-permute-done | bytes 1376288 | tf_op jit(solution)/shard_map/ppermute | solution.py:25
  371.6 33.3 %collective-permute-done.23 = bf16[1280,672]{0,1:T(8,128)(2,1)S(1)} collective-permute-done((bf16[1280,672]{0,1:T(8,128)(2,1)S(1)}, bf16[1280,672]{0,1:T(8,128)(2,1)S(1)}, u32[]{:S(2)}, u32[]{:S(2)}) %collective-permute-start.23) | collective-permute-done | bytes 1720352 | tf_op jit(solution)/shard_map/ppermute | solution.py:25
  405.9 31.4 %collective-permute-done.24 = bf16[1280,672]{0,1:T(8,128)(2,1)S(1)} collective-permute-done((bf16[1280,672]{0,1:T(8,128)(2,1)S(1)}, bf16[1280,672]{0,1:T(8,128)(2,1)S(1)}, u32[]{:S(2)}, u32[]{:S(2)}) %collective-permute-start.24) | collective-permute-done | bytes 1720352 | tf_op jit(solution)/shard_map/ppermute | solution.py:25
  447.9 4.6 copy.58
  452.6 52.7 %reduce-scatter.4.cloned.1.call-done = bf16[128,2688]{1,0:T(8,128)(2,1)} async-done(((bf16[512,2688]{1,0:T(8,128)(2,1)}), bf16[128,2688]{1,0:T(8,128)(2,1)}) %reduce-scatter.4.cloned.1.call-update) | async-done | bytes 688144 | tf_op jit(solution)/shard_map/reduce_scatter | solution.py:188
  (160 shorter events, 77.5 us)
Async XLA Ops:
  6.5 498.7 %reduce-scatter.4.cloned.1.call-start = ((), (), s32[]{:S(2)}) async-start(), calls=%async_computation.1 | async-start | bytes 3440640 | tf_op jit(solution)/shard_map/reduce_scatter | solution.py:188
  36.8 56.6 %collective-permute-start.3 = (bf16[768,672]{0,1:T(8,128)(2,1)}, bf16[768,672]{0,1:T(8,128)(2,1)}, u32[]{:S(2)}, u32[]{:S(2)}) collective-permute-start(bf16[768,672]{0,1:T(8,128)(2,1)} %multiply_convert_fusion.2), channel_id=1, source_target_pairs={{0,1},{1,0},{2,3},{3,2},{4,5},{5,4},{6,7},{7,6},{8,9},{9,8},{10,11... | collective-permute-start | bytes 3096584 | tf_op jit(solution)/shard_map/ppermute | solution.py:25
  51.0 59.9 %collective-permute-start = (bf16[512,2,512]{0,2,1:T(8,128)(2,1)}, bf16[512,2,512]{0,2,1:T(8,128)(2,1)}, u32[]{:S(2)}, u32[]{:S(2)}) collective-permute-start(bf16[512,2,512]{0,2,1:T(8,128)(2,1)} %pad_maximum_fusion.11), channel_id=1, source_target_pairs={{0,4},{4,8},{8,12},{1,5},{5,9},{9,13},{2,6},{6,10},{10,14},{3,7},{... | collective-permute-start | bytes 3145736 | tf_op jit(solution)/shard_map/ppermute | solution.py:21
  54.7 70.1 %collective-permute-start.2 = (bf16[512,672]{0,1:T(8,128)(2,1)}, bf16[512,672]{0,1:T(8,128)(2,1)}, u32[]{:S(2)}, u32[]{:S(2)}) collective-permute-start(bf16[512,672]{0,1:T(8,128)(2,1)} %constant_dynamic-slice_fusion), channel_id=1, source_target_pairs={{0,16},{16,0},{1,17},{17,1},{2,18},{18,2},{3,19},{19,3},{4,20},{20... | collective-permute-start | bytes 2064392 | tf_op jit(solution)/shard_map/ppermute | solution.py:25
  93.5 39.7 %collective-permute-start.6 = (bf16[640,672]{0,1:T(8,128)(2,1)}, bf16[640,672]{0,1:T(8,128)(2,1)}, u32[]{:S(2)}, u32[]{:S(2)}) collective-permute-start(bf16[640,672]{0,1:T(8,128)(2,1)} %get-tuple-element.8), channel_id=1, source_target_pairs={{0,1},{1,0},{2,3},{3,2},{4,5},{5,4},{6,7},{7,6},{8,9},{9,8},{10,11... | collective-permute-start | bytes 2580488 | tf_op jit(solution)/shard_map/ppermute | solution.py:25
  96.0 49.0 %collective-permute-start.4 = (bf16[768,672]{0,1:T(8,128)(2,1)S(1)}, bf16[768,672]{0,1:T(8,128)(2,1)}, u32[]{:S(2)}, u32[]{:S(2)}) collective-permute-start(bf16[768,672]{0,1:T(8,128)(2,1)S(1)} %fusion.18), channel_id=1, source_target_pairs={{0,2},{1,3},{2,0},{3,1},{4,6},{5,7},{6,4},{7,5},{8,10},{9,11},{10,... | collective-permute-start | bytes 3096584 | tf_op jit(solution)/shard_map/ppermute | solution.py:25
  110.9 37.3 %collective-permute-start.1 = (bf16[512,2,512]{0,2,1:T(8,128)(2,1)}, bf16[512,2,512]{0,2,1:T(8,128)(2,1)}, u32[]{:S(2)}, u32[]{:S(2)}) collective-permute-start(bf16[512,2,512]{0,2,1:T(8,128)(2,1)} %collective-permute-done), channel_id=1, source_target_pairs={{0,4},{4,8},{8,12},{1,5},{5,9},{9,13},{2,6},{6,10},{10,14},{3,7},{... | collective-permute-start | bytes 3145736 | tf_op jit(solution)/shard_map/ppermute | solution.py:21
  127.4 176.6 %collective-permute-start.15 = (bf16[1024,672]{0,1:T(8,128)(2,1)}, bf16[1024,672]{0,1:T(8,128)(2,1)}, u32[]{:S(2)}, u32[]{:S(2)}) collective-permute-start(bf16[1024,672]{0,1:T(8,128)(2,1)} %pad_maximum_fusion.7), channel_id=1, source_target_pairs={{0,4},{4,0},{8,12},{12,8},{1,5},{5,1},{9,13},{13,9},{2,6},{6,2},{1... | collective-permute-start | bytes 4128776 | tf_op jit(solution)/shard_map/ppermute | solution.py:25
  133.2 56.8 %collective-permute-start.9 = (bf16[640,672]{0,1:T(8,128)(2,1)}, bf16[640,672]{0,1:T(8,128)(2,1)}, u32[]{:S(2)}, u32[]{:S(2)}) collective-permute-start(bf16[640,672]{0,1:T(8,128)(2,1)} %get-tuple-element.9), channel_id=1, source_target_pairs={{0,1},{1,0},{2,3},{3,2},{4,5},{5,4},{6,7},{7,6},{8,9},{9,8},{10,11... | collective-permute-start | bytes 2580488 | tf_op jit(solution)/shard_map/ppermute | solution.py:25
  135.8 61.0 %collective-permute-start.7 = (bf16[640,672]{0,1:T(8,128)(2,1)}, bf16[640,672]{0,1:T(8,128)(2,1)}, u32[]{:S(2)}, u32[]{:S(2)}) collective-permute-start(bf16[640,672]{0,1:T(8,128)(2,1)} %fusion.22), channel_id=1, source_target_pairs={{0,2},{1,3},{2,0},{3,1},{4,6},{5,7},{6,4},{7,5},{8,10},{9,11},{10,... | collective-permute-start | bytes 2580488 | tf_op jit(solution)/shard_map/ppermute | solution.py:25
  147.6 52.5 %collective-permute-start.5 = (bf16[768,672]{0,1:T(8,128)(2,1)}, bf16[768,672]{0,1:T(8,128)(2,1)}, u32[]{:S(2)}, u32[]{:S(2)}) collective-permute-start(bf16[768,672]{0,1:T(8,128)(2,1)} %fusion.20), channel_id=1, source_target_pairs={{0,16},{16,0},{1,17},{17,1},{2,18},{18,2},{3,19},{19,3},{4,20},{20... | collective-permute-start | bytes 3096584 | tf_op jit(solution)/shard_map/ppermute | solution.py:25
  191.0 36.6 %collective-permute-start.12 = (bf16[640,672]{0,1:T(8,128)(2,1)S(1)}, bf16[640,672]{0,1:T(8,128)(2,1)S(1)}, u32[]{:S(2)}, u32[]{:S(2)}) collective-permute-start(bf16[640,672]{0,1:T(8,128)(2,1)S(1)} %copy-done.10), channel_id=1, source_target_pairs={{0,1},{1,0},{2,3},{3,2},{4,5},{5,4},{6,7},{7,6},{8,9},{9,8},{10,11... | collective-permute-start | bytes 2580488 | tf_op jit(solution)/shard_map/ppermute | solution.py:25
  193.2 60.5 %collective-permute-start.10 = (bf16[640,672]{0,1:T(8,128)(2,1)S(1)}, bf16[640,672]{0,1:T(8,128)(2,1)S(1)}, u32[]{:S(2)}, u32[]{:S(2)}) collective-permute-start(bf16[640,672]{0,1:T(8,128)(2,1)S(1)} %fusion.26), channel_id=1, source_target_pairs={{0,2},{1,3},{2,0},{3,1},{4,6},{5,7},{6,4},{7,5},{8,10},{9,11},{10,... | collective-permute-start | bytes 2580488 | tf_op jit(solution)/shard_map/ppermute | solution.py:25
  198.6 55.5 %collective-permute-start.8 = (bf16[640,672]{0,1:T(8,128)(2,1)S(1)}, bf16[640,672]{0,1:T(8,128)(2,1)S(1)}, u32[]{:S(2)}, u32[]{:S(2)}) collective-permute-start(bf16[640,672]{0,1:T(8,128)(2,1)S(1)} %fusion.24), channel_id=1, source_target_pairs={{0,16},{16,0},{1,17},{17,1},{2,18},{18,2},{3,19},{19,3},{4,20},{20... | collective-permute-start | bytes 2580488 | tf_op jit(solution)/shard_map/ppermute | solution.py:25
  201.7 70.6 %collective-permute-start.16 = (bf16[1536,672]{0,1:T(8,128)(2,1)S(1)}, bf16[1536,672]{0,1:T(8,128)(2,1)S(1)}, u32[]{:S(2)}, u32[]{:S(2)}) collective-permute-start(bf16[1536,672]{0,1:T(8,128)(2,1)S(1)} %pad_maximum_fusion.2), channel_id=1, source_target_pairs={{0,4},{4,0},{8,12},{12,8},{1,5},{5,1},{9,13},{13,9},{2,6},{6,2},{1... | collective-permute-start | bytes 6193160 | tf_op jit(solution)/shard_map/ppermute | solution.py:25
  228.0 42.5 %collective-permute-start.13 = (bf16[640,672]{0,1:T(8,128)(2,1)S(1)}, bf16[640,672]{0,1:T(8,128)(2,1)S(1)}, u32[]{:S(2)}, u32[]{:S(2)}) collective-permute-start(bf16[640,672]{0,1:T(8,128)(2,1)S(1)} %fusion.30), channel_id=1, source_target_pairs={{0,2},{1,3},{2,0},{3,1},{4,6},{5,7},{6,4},{7,5},{8,10},{9,11},{10,... | collective-permute-start | bytes 2580488 | tf_op jit(solution)/shard_map/ppermute | solution.py:25
  253.7 47.9 %collective-permute-start.21 = (bf16[1536,672]{0,1:T(8,128)(2,1)S(1)}, bf16[1536,672]{0,1:T(8,128)(2,1)S(1)}, u32[]{:S(2)}, u32[]{:S(2)}) collective-permute-start(bf16[1536,672]{0,1:T(8,128)(2,1)S(1)} %pad_maximum_fusion.2), channel_id=1, source_target_pairs={{0,8},{4,12},{8,0},{12,4},{1,9},{5,13},{9,1},{13,5},{2,10},{6,14},... | collective-permute-start | bytes 6193160 | tf_op jit(solution)/shard_map/ppermute | solution.py:25
  254.1 18.0 %collective-permute-start.11 = (bf16[640,672]{0,1:T(8,128)(2,1)S(1)}, bf16[640,672]{0,1:T(8,128)(2,1)S(1)}, u32[]{:S(2)}, u32[]{:S(2)}) collective-permute-start(bf16[640,672]{0,1:T(8,128)(2,1)S(1)} %fusion.28), channel_id=1, source_target_pairs={{0,16},{16,0},{1,17},{17,1},{2,18},{18,2},{3,19},{19,3},{4,20},{20... | collective-permute-start | bytes 2580488 | tf_op jit(solution)/shard_map/ppermute | solution.py:25
  270.8 30.8 %collective-permute-start.14 = (bf16[640,672]{0,1:T(8,128)(2,1)S(1)}, bf16[640,672]{0,1:T(8,128)(2,1)S(1)}, u32[]{:S(2)}, u32[]{:S(2)}) collective-permute-start(bf16[640,672]{0,1:T(8,128)(2,1)S(1)} %fusion.32), channel_id=1, source_target_pairs={{0,16},{16,0},{1,17},{17,1},{2,18},{18,2},{3,19},{19,3},{4,20},{20... | collective-permute-start | bytes 2580488 | tf_op jit(solution)/shard_map/ppermute | solution.py:25
  272.1 34.0 %collective-permute-start.17 = (bf16[1280,672]{0,1:T(8,128)(2,1)S(1)}, bf16[1280,672]{0,1:T(8,128)(2,1)S(1)}, u32[]{:S(2)}, u32[]{:S(2)}) collective-permute-start(bf16[1280,672]{0,1:T(8,128)(2,1)S(1)} %pad_maximum_fusion.3), channel_id=1, source_target_pairs={{0,4},{4,0},{8,12},{12,8},{1,5},{5,1},{9,13},{13,9},{2,6},{6,2},{1... | collective-permute-start | bytes 5160968 | tf_op jit(solution)/shard_map/ppermute | solution.py:25
  272.3 66.1 %collective-permute-start.22 = (bf16[1280,672]{0,1:T(8,128)(2,1)S(1)}, bf16[1280,672]{0,1:T(8,128)(2,1)S(1)}, u32[]{:S(2)}, u32[]{:S(2)}) collective-permute-start(bf16[1280,672]{0,1:T(8,128)(2,1)S(1)} %pad_maximum_fusion.3), channel_id=1, source_target_pairs={{0,8},{4,12},{8,0},{12,4},{1,9},{5,13},{9,1},{13,5},{2,10},{6,14},... | collective-permute-start | bytes 5160968 | tf_op jit(solution)/shard_map/ppermute | solution.py:25
  301.6 66.4 %collective-permute-start.20 = (bf16[1024,672]{0,1:T(8,128)(2,1)}, bf16[1024,672]{0,1:T(8,128)(2,1)S(1)}, u32[]{:S(2)}, u32[]{:S(2)}) collective-permute-start(bf16[1024,672]{0,1:T(8,128)(2,1)} %pad_maximum_fusion.7), channel_id=1, source_target_pairs={{0,8},{4,12},{8,0},{12,4},{1,9},{5,13},{9,1},{13,5},{2,10},{6,14},... | collective-permute-start | bytes 4128776 | tf_op jit(solution)/shard_map/ppermute | solution.py:25
  301.6 67.4 %collective-permute-start.18 = (bf16[1280,672]{0,1:T(8,128)(2,1)S(1)}, bf16[1280,672]{0,1:T(8,128)(2,1)S(1)}, u32[]{:S(2)}, u32[]{:S(2)}) collective-permute-start(bf16[1280,672]{0,1:T(8,128)(2,1)S(1)} %pad_maximum_fusion.4), channel_id=1, source_target_pairs={{0,4},{4,0},{8,12},{12,8},{1,5},{5,1},{9,13},{13,9},{2,6},{6,2},{1... | collective-permute-start | bytes 5160968 | tf_op jit(solution)/shard_map/ppermute | solution.py:25
  303.9 100.9 %collective-permute-start.23 = (bf16[1280,672]{0,1:T(8,128)(2,1)S(1)}, bf16[1280,672]{0,1:T(8,128)(2,1)S(1)}, u32[]{:S(2)}, u32[]{:S(2)}) collective-permute-start(bf16[1280,672]{0,1:T(8,128)(2,1)S(1)} %pad_maximum_fusion.4), channel_id=1, source_target_pairs={{0,8},{4,12},{8,0},{12,4},{1,9},{5,13},{9,1},{13,5},{2,10},{6,14},... | collective-permute-start | bytes 5160968 | tf_op jit(solution)/shard_map/ppermute | solution.py:25
  306.2 131.1 %collective-permute-start.24 = (bf16[1280,672]{0,1:T(8,128)(2,1)S(1)}, bf16[1280,672]{0,1:T(8,128)(2,1)S(1)}, u32[]{:S(2)}, u32[]{:S(2)}) collective-permute-start(bf16[1280,672]{0,1:T(8,128)(2,1)S(1)} %pad_maximum_fusion.5), channel_id=1, source_target_pairs={{0,8},{4,12},{8,0},{12,4},{1,9},{5,13},{9,1},{13,5},{2,10},{6,14},... | collective-permute-start | bytes 5160968 | tf_op jit(solution)/shard_map/ppermute | solution.py:25
  338.5 99.9 %collective-permute-start.27 = (bf16[1280,672]{0,1:T(8,128)(2,1)S(1)}, bf16[1280,672]{0,1:T(8,128)(2,1)S(1)}, u32[]{:S(2)}, u32[]{:S(2)}) collective-permute-start(bf16[1280,672]{0,1:T(8,128)(2,1)S(1)} %collective-permute-done.22), channel_id=1, source_target_pairs={{0,4},{4,0},{8,12},{12,8},{1,5},{5,1},{9,13},{13,9},{2,6},{6,2},{1... | collective-permute-start | bytes 5160968 | tf_op jit(solution)/shard_map/ppermute | solution.py:25
  368.0 72.0 %collective-permute-start.19 = (bf16[1280,672]{0,1:T(8,128)(2,1)S(1)}, bf16[1280,672]{0,1:T(8,128)(2,1)S(1)}, u32[]{:S(2)}, u32[]{:S(2)}) collective-permute-start(bf16[1280,672]{0,1:T(8,128)(2,1)S(1)} %pad_maximum_fusion.5), channel_id=1, source_target_pairs={{0,4},{4,0},{8,12},{12,8},{1,5},{5,1},{9,13},{13,9},{2,6},{6,2},{1... | collective-permute-start | bytes 5160968 | tf_op jit(solution)/shard_map/ppermute | solution.py:25
  369.0 72.3 %collective-permute-start.26 = (bf16[1536,672]{0,1:T(8,128)(2,1)S(1)}, bf16[1536,672]{0,1:T(8,128)(2,1)S(1)}, u32[]{:S(2)}, u32[]{:S(2)}) collective-permute-start(bf16[1536,672]{0,1:T(8,128)(2,1)S(1)} %collective-permute-done.21), channel_id=1, source_target_pairs={{0,4},{4,0},{8,12},{12,8},{1,5},{5,1},{9,13},{13,9},{2,6},{6,2},{1... | collective-permute-start | bytes 6193160 | tf_op jit(solution)/shard_map/ppermute | solution.py:25
  404.8 37.8 %collective-permute-start.25 = (bf16[1024,672]{0,1:T(8,128)(2,1)S(1)}, bf16[1024,672]{0,1:T(8,128)(2,1)S(1)}, u32[]{:S(2)}, u32[]{:S(2)}) collective-permute-start(bf16[1024,672]{0,1:T(8,128)(2,1)S(1)} %collective-permute-done.20), channel_id=1, source_target_pairs={{0,4},{4,0},{8,12},{12,8},{1,5},{5,1},{9,13},{13,9},{2,6},{6,2},{1... | collective-permute-start | bytes 4128776 | tf_op jit(solution)/shard_map/ppermute | solution.py:25
  437.3 6.2 %collective-permute-start.28 = (bf16[1280,672]{0,1:T(8,128)(2,1)S(1)}, bf16[1280,672]{0,1:T(8,128)(2,1)S(1)}, u32[]{:S(2)}, u32[]{:S(2)}) collective-permute-start(bf16[1280,672]{0,1:T(8,128)(2,1)S(1)} %collective-permute-done.23), channel_id=1, source_target_pairs={{0,4},{4,0},{8,12},{12,8},{1,5},{5,1},{9,13},{13,9},{2,6},{6,2},{1... | collective-permute-start | bytes 5160968 | tf_op jit(solution)/shard_map/ppermute | solution.py:25
  438.4 6.2 %collective-permute-start.29 = (bf16[1280,672]{0,1:T(8,128)(2,1)S(1)}, bf16[1280,672]{0,1:T(8,128)(2,1)S(1)}, u32[]{:S(2)}, u32[]{:S(2)}) collective-permute-start(bf16[1280,672]{0,1:T(8,128)(2,1)S(1)} %collective-permute-done.24), channel_id=1, source_target_pairs={{0,4},{4,0},{8,12},{12,8},{1,5},{5,1},{9,13},{13,9},{2,6},{6,2},{1... | collective-permute-start | bytes 5160968 | tf_op jit(solution)/shard_map/ppermute | solution.py:25
  447.9 57.4 %copy-start.1 = (bf16[1024,672]{0,1:T(8,128)(2,1)S(1)}, bf16[1024,672]{0,1:T(8,128)(2,1)}, u32[]{:S(2)}) copy-start(bf16[1024,672]{0,1:T(8,128)(2,1)} %param.16) | copy-start | bytes 4128772
  (26 other events, 289.6 us)
Sparse Core Ops, SparseCore 0:
  452.7 52.5 reduce-scatter.3

commit v3 on v2

--- a/solution.py
+++ b/solution.py
@@ -40,12 +40,22 @@
     )
 
 
-def gathered(piece):
-    held = {0: jnp.concatenate([piece, swapped(piece, "group", 0)], axis=0)}
-    for bit_index in reversed(range(lax.axis_size("seq").bit_length() - 1)):
+def both_groups(piece):
+    return jnp.concatenate([piece, swapped(piece, "group", 0)], axis=0)
+
+
+def spread(held, bits):
+    for bit_index in bits:
         for distance, columns in list(held.items()):
             held[distance | 1 << bit_index] = swapped(columns, "seq", bit_index)
     return held
+
+
+def over_chips(piece, seq_first):
+    bits = list(reversed(range(1, lax.axis_size("seq").bit_length() - 1)))
+    if seq_first:
+        return {d: both_groups(part) for d, part in spread({0: piece}, bits).items()}
+    return spread({0: both_groups(piece)}, bits)
 
 
 def own_and_other(rows, group_index, begin, count, half):
@@ -148,23 +158,34 @@
 
     half = rotated.shape[1] // 2
     out_half = out_weight.shape[0] // 2
-    scale_rows = jnp.repeat(down_scales, GROUP, axis=0)
     unit = half // 21
     out_piece = lax.dynamic_slice_in_dim(out_weight, group_index * out_half, out_half, 0)
     tokens_left = own_and_other(attended, group_index, 0, out_half, out_half)
-    totals = {
-        distance: jnp.dot(tokens_left, columns, preferred_element_type=jnp.float32)
-        for distance, columns in gathered(out_piece).items()
-    }
+    out_wide = over_chips(out_piece, True)
+    wides = []
+    lefts = []
     tied = None
-    for first, last in ((0, 6), (6, 11), (11, 16), (16, 21)):
+    for chunk, (first, last) in enumerate(((0, 6), (6, 12), (12, 17), (17, 21))):
         begin, rows = first * unit, (last - first) * unit
         codes = lax.dynamic_slice_in_dim(down_codes, group_index * half + begin, rows, 0)
-        scales = lax.dynamic_slice_in_dim(scale_rows, group_index * half + begin, rows, 0)
+        if unit % GROUP == 0:
+            scales = lax.dynamic_slice_in_dim(
+                down_scales, (group_index * half + begin) // GROUP, rows // GROUP, 0
+            )
+            codes = codes.reshape(rows // GROUP, GROUP, codes.shape[1])
+            scales = scales[:, None, :]
+        else:
+            scale_rows = jnp.repeat(down_scales, GROUP, axis=0)
+            scales = lax.dynamic_slice_in_dim(scale_rows, group_index * half + begin, rows, 0)
         piece = (((codes - 8) * scales).astype(jnp.float32) * CODE_STEP).astype(jnp.bfloat16)
+        piece = piece.reshape(rows, piece.shape[-1])
         for bit_index in range(tp_count.bit_length() - 1):
             if bit_index == 0 and tied is not None:
                 piece, tied = lax.optimization_barrier((piece, tied))
+            if bit_index == 1 and chunk == 1:
+                piece, out_wide = lax.optimization_barrier((piece, out_wide))
+            if bit_index == 1 and chunk == 3:
+                piece, wides[0] = lax.optimization_barrier((piece, wides[0]))
             partner = swapped(piece, "tp", bit_index)
             if bit_index == 0:
                 tied = partner
@@ -174,8 +195,14 @@
             piece = jnp.where(
                 high_side == 0, own_values + other_values, other_values - own_values
             ).astype(jnp.bfloat16)
-        left = own_and_other(rotated, group_index, begin, rows, half)
-        for distance, columns in gathered(piece).items():
+        lefts.append(own_and_other(rotated, group_index, begin, rows, half))
+        wides.append(over_chips(piece, chunk < 2))
+    totals = {
+        distance: jnp.dot(tokens_left, columns, preferred_element_type=jnp.float32)
+        for distance, columns in spread(out_wide, [0]).items()
+    }
+    for left, wide in zip(lefts, wides):
+        for distance, columns in spread(wide, [0]).items():
             totals[distance] += jnp.dot(left, columns, preferred_element_type=jnp.float32)
     stacked = jnp.stack([totals[d].astype(jnp.bfloat16) for d in sorted(totals)])
     partials = jnp.concatenate(

time: 521 us -> 443 us (0.85)
  waiting for transfers between devices: 272 us -> 162 us
  other arithmetic: 52 us -> 70.9 us
  matrix products: 88.9 us -> 103 us
  local copies, waits for them, and re-layouts: 52.6 us -> 58.1 us
    ppermute x28 -> x31, waiting for transfers between devices: 219 us -> 110 us  [swapped(): lax.ppermute(x, axis, [(i, i ^ 1 << stride) for i in range(lax.axis_size(...]
    unnamed x60 -> x80, local copies, waits for them, and re-layouts: 35.3 us -> 21.2 us
    dot_general x16, matrix products: 19.3 us -> 33.3 us  [per_device(): jnp.dot(left, columns, preferred_element_type=jnp.float32)]
    concatenate x5 -> x7, other arithmetic: 4.59 us -> 17.2 us  [both_groups(): return jnp.concatenate([piece, swapped(piece, 'group', 0)], axis=0)]
    mul x0 -> x5, local copies, waits for them, and re-layouts: none -> 9.28 us  [per_device(): (codes - 8) * scales]
    broadcast_in_dim x1 -> x0, local copies, waits for them, and re-layouts: 7.87 us -> none  [per_device(): scale_rows = jnp.repeat(down_scales, GROUP, axis=0)]
    convert_element_type x8, other arithmetic: 11.7 us -> 18.1 us  [per_device(): piece = jnp.where(high_side == 0, own_values + other_values, other_values...]
    concatenate x0 -> x2, local copies, waits for them, and re-layouts: none -> 6.32 us  [both_groups(): return jnp.concatenate([piece, swapped(piece, 'group', 0)], axis=0)]
  transfers between devices with their start and end apart: 31 -> 34, of which waited for: 11 -> 10; matrix products, arithmetic and copies ran while one was open for 30% -> 50% of each run, Pallas kernels for 0% -> 0%
where the time goes in v3:
time: 443 us; the launch traced here: 438 us
  waiting for transfers between devices  162 us (37%)
  matrix products  103 us (23%)
  other arithmetic  70.9 us (16%)
  local copies, waits for them, and re-layouts  58.1 us (13%)
  starting transfers between devices  29.1 us (7%)
  between operations  15.1 us (3%)
    ppermute x31, waiting for transfers between devices, swapped(): lax.ppermute(x, axis, [(i, i ^ 1 << stride) for i in range(lax.axis_size(...  110 us
    reduce_scatter x1, waiting for transfers between devices, per_device(): return lax.psum_scatter(partials, 'tp', scatter_dimension=0, tiled=True)  51.7 us
    dot_general x16, matrix products, per_device(): jnp.dot(left, columns, preferred_element_type=jnp.float32)  33.3 us
    dot_general x2, matrix products, per_device(): jnp.dot(hidden[:, first:first + width], mixer, preferred_element_type=jnp...  27.8 us
    ppermute x31, starting transfers between devices, swapped(): lax.ppermute(x, axis, [(i, i ^ 1 << stride) for i in range(lax.axis_size(...  24.4 us
    unnamed x80, local copies, waits for them, and re-layouts  21.2 us
    convert_element_type x8, other arithmetic, per_device(): piece = jnp.where(high_side == 0, own_values + other_values, other_values...  18.1 us
    concatenate x7, other arithmetic, both_groups(): return jnp.concatenate([piece, swapped(piece, 'group', 0)], axis=0)  17.2 us
  transfers between devices with their start and end apart: 34, of which 10 were waited for; matrix products, arithmetic and copies ran while one was open for 50% of the time, Pallas kernels for 0%

profile of v3, /device:TPU:0, one launch (start us, length us, event | category | flops | bytes accessed | tf_op | source)
XLA Modules:
  0.0 437.6 jit_solution(9947269569653999502)
XLA Ops:
  8.8 3.0 collective-permute-start.5
  19.2 3.0 copy.85
  22.2 4.9 %multiply_convert_fusion.2 = (bf16[768,672]{0,1:T(8,128)(2,1)}, bf16[768,672]{0,1:T(8,128)(2,1)}) fusion(s32[768,672]{0,1:T(8,128)} %copy.85, s32[5376,672]{0,1:T(8,128)} %param.14, s32[]{:T(128)S(6)} %select_n.171, s32[768,672]{0,1:T(8,128)S(1)} %copy.84, s32[]{:T(128)S(6)} %select_n.168), kind=kLoop, calls=%fused_computation.71 | loop fusion | flops 5160960 | bytes 10321928 | tf_op jit(solution)/shard_map/convert_element_type | solution.py:180
  37.3 11.8 %fusion.11 = f32[2688,512]{1,0:T(8,128)S(1)} fusion(bf16[2688,2688]{1,0:T(8,128)(2,1)} %constant.159.clone, bf16[512,5376]{1,0:T(8,128)(2,1)} %param.13), kind=kOutput, calls=%fused_computation.39 | convolution fusion | flops 7398752256 | bytes 22708224 | tf_op jit(solution)/shard_map/dot_general | solution.py:147
  49.1 16.0 %fusion.10 = (bf16[512,2688]{0,1:T(8,128)(2,1)}, bf16[512,2688]{0,1:T(8,128)(2,1)}) fusion(f32[2688,512]{1,0:T(8,128)S(1)} %fusion.11, bf16[2688,2688]{1,0:T(8,128)(2,1)} %constant.159.clone, bf16[512,5376]{1,0:T(8,128)(2,1)} %param.13), kind=kOutput, calls=%fused_computation.36 | convolution fusion | flops 7407009792 | bytes 28213248 | tf_op jit(solution)/shard_map/dot_general | solution.py:147
  80.4 5.5 %fusion.43 = (bf16[512,768]{0,1:T(8,128)(2,1)}, bf16[512,768]{0,1:T(8,128)(2,1)}, bf16[512,768]{0,1:T(8,128)(2,1)}, bf16[512,768]{0,1:T(8,128)(2,1)}) fusion(s32[]{:T(128)S(6)} %select_n.171, bf16[512,2688]{0,1:T(8,128)(2,1)} %get-tuple-element.26, bf16[512,2688]{0,1:T(8,128)(2,1)} %get-tuple-element.25, s32[]{:T(128)S(6)} %select_n.175, s32[]{:T(128)S(6)} %select_n.168, ...), kind=kLoop, calls=%fused_computation.114 | loop fusion | flops 6291456 | bytes 8650768 | tf_op jit(solution)/shard_map/concatenate | solution.py:157
  89.7 3.1 fusion.53
  92.8 4.7 %copy.76 = bf16[1024,2,512]{0,2,1:T(8,128)(2,1)} copy(bf16[1024,2,512]{2,1,0:T(2,128)(2,1)S(1)} %copy-done.11) | data formatting | bytes 4194304 | tf_op args[2]
  97.5 3.4 fusion.16
  104.0 3.3 copy.109
  109.1 3.3 fusion.50
  117.6 8.5 %collective-permute-done.9 = bf16[768,672]{0,1:T(8,128)(2,1)} collective-permute-done((bf16[768,672]{0,1:T(8,128)(2,1)}, bf16[768,672]{0,1:T(8,128)(2,1)}, u32[]{:S(2)}, u32[]{:S(2)}) %collective-permute-start.9) | collective-permute-done | bytes 1032224 | tf_op jit(solution)/shard_map/ppermute | solution.py:25
  129.5 6.5 %collective-permute-done.3 = bf16[768,672]{0,1:T(8,128)(2,1)} collective-permute-done((bf16[768,672]{0,1:T(8,128)(2,1)}, bf16[768,672]{0,1:T(8,128)(2,1)}, u32[]{:S(2)}, u32[]{:S(2)}) %collective-permute-start.3) | collective-permute-done | bytes 1032224 | tf_op jit(solution)/shard_map/ppermute | solution.py:25
  145.3 12.0 %fusion.54 = f32[4,1536,512,2]{2,1,3,0:T(8,128)} fusion(bf16[1536,4,128,1]{0,2,3,1:T(8,128)(2,1)S(1)} %bitcast.105, bf16[512,4,2,64]{3,0,2,1:T(8,128)(2,1)S(1)} %bitcast.113, bf16[512,4,2,64]{3,0,2,1:T(8,128)(2,1)S(1)} %bitcast.111), kind=kOutput, calls=%fused_computation.135 | convolution fusion | flops 1612709888 | bytes 27787264 | tf_op jit(solution)/shard_map/qkgd,skd->kgqs/dot_general | solution.py:127
  157.3 10.3 %fusion.84 = f32[4,2,512]{2,1,0:T(2,128)S(1)} fusion(pred[512,1536]{0,1:T(8,128)(4,1)} %fusion.8, bf16[1536,4,128,1]{0,2,3,1:T(8,128)(2,1)S(1)} %bitcast.106, bf16[512,4,2,64]{3,0,2,1:T(8,128)(2,1)} %bitcast.112, bf16[512,4,2,64]{3,0,2,1:T(8,128)(2,1)} %bitcast.110), kind=kOutput, calls=%fused_computation.175 | convolution fusion | flops 1637877248 | bytes 3424256 | tf_op jit(solution)/shard_map/sub | solution.py:135
  167.7 14.5 %fusion.32 = bf16[4,128,2,512]{3,1,2,0:T(8,128)(2,1)} fusion(bf16[1536,4,128,1]{0,2,3,1:T(8,128)(2,1)} %bitcast.115, f32[4,2,512]{2,1,0:T(2,128)S(1)} %fusion.84, f32[4,1536,512,2]{2,1,3,0:T(8,128)} %fusion.54, pred[512,1536]{0,1:T(8,128)(4,1)} %fusion.8), kind=kOutput, calls=%fused_computation.88 | convolution fusion | flops 1642599936 | bytes 28590080 | tf_op jit(solution)/shard_map/kgqs,skd->qkgd/dot_general | solution.py:139
  200.6 3.0 pad_maximum_fusion.2
  203.6 8.0 %collective-permute-done.8 = bf16[512,672]{0,1:T(8,128)(2,1)} collective-permute-done((bf16[512,672]{0,1:T(8,128)(2,1)}, bf16[512,672]{0,1:T(8,128)(2,1)}, u32[]{:S(2)}, u32[]{:S(2)}) %collective-permute-start.8) | collective-permute-done | bytes 688160 | tf_op jit(solution)/shard_map/ppermute | solution.py:25
  214.0 17.8 %collective-permute-done.15 = bf16[640,672]{0,1:T(8,128)(2,1)S(1)} collective-permute-done((bf16[640,672]{0,1:T(8,128)(2,1)}, bf16[640,672]{0,1:T(8,128)(2,1)S(1)}, u32[]{:S(2)}, u32[]{:S(2)}) %collective-permute-start.15) | collective-permute-done | bytes 860192 | tf_op jit(solution)/shard_map/ppermute | solution.py:25
  237.7 3.0 pad_maximum_fusion.3
  240.9 3.0 collective-permute-done.14
  243.9 3.0 pad_maximum_fusion.4
  246.9 3.9 fusion.77
  250.9 4.0 fusion.79
  256.4 3.8 fusion.74
  260.2 10.3 %collective-permute-done.17 = bf16[512,672]{0,1:T(8,128)(2,1)S(1)} collective-permute-done((bf16[512,672]{0,1:T(8,128)(2,1)S(1)}, bf16[512,672]{0,1:T(8,128)(2,1)S(1)}, u32[]{:S(2)}, u32[]{:S(2)}) %collective-permute-start.17) | collective-permute-done | bytes 688160 | tf_op jit(solution)/shard_map/ppermute | solution.py:25
  281.0 4.0 copy.94
  287.9 8.0 %collective-permute-done.18 = bf16[512,672]{0,1:T(8,128)(2,1)} collective-permute-done((bf16[512,672]{0,1:T(8,128)(2,1)}, bf16[512,672]{0,1:T(8,128)(2,1)}, u32[]{:S(2)}, u32[]{:S(2)}) %collective-permute-start.18) | collective-permute-done | bytes 688160 | tf_op jit(solution)/shard_map/ppermute | solution.py:25
  313.9 22.7 %collective-permute-done.26 = bf16[1280,672]{0,1:T(8,128)(2,1)S(1)} collective-permute-done((bf16[1280,672]{0,1:T(8,128)(2,1)}, bf16[1280,672]{0,1:T(8,128)(2,1)S(1)}, u32[]{:S(2)}, u32[]{:S(2)}) %collective-permute-start.26) | collective-permute-done | bytes 1720352 | tf_op jit(solution)/shard_map/ppermute | solution.py:25
  339.3 25.2 %collective-permute-done.27 = bf16[1024,672]{0,1:T(8,128)(2,1)S(1)} collective-permute-done((bf16[1024,672]{0,1:T(8,128)(2,1)S(1)}, bf16[1024,672]{0,1:T(8,128)(2,1)S(1)}, u32[]{:S(2)}, u32[]{:S(2)}) %collective-permute-start.27) | collective-permute-done | bytes 1376288 | tf_op jit(solution)/shard_map/ppermute | solution.py:25
  374.2 4.6 %copy.102 = bf16[512,2688]{1,0:T(8,128)(2,1)} copy(bf16[512,2688]{0,1:T(8,128)(2,1)} %pad_maximum_fusion.1) | data formatting | bytes 5505024
  378.8 51.7 %reduce-scatter.4.cloned.1.call-done = bf16[128,2688]{1,0:T(8,128)(2,1)} async-done(((bf16[512,2688]{1,0:T(8,128)(2,1)}), bf16[128,2688]{1,0:T(8,128)(2,1)}) %reduce-scatter.4.cloned.1.call-update) | async-done | bytes 688144 | tf_op jit(solution)/shard_map/reduce_scatter | solution.py:215
  (206 shorter events, 132.6 us)
Async XLA Ops:
  6.5 423.9 %reduce-scatter.4.cloned.1.call-start = ((), (), s32[]{:S(2)}) async-start(), calls=%async_computation.1 | async-start | bytes 3440640 | tf_op jit(solution)/shard_map/reduce_scatter | solution.py:215
  8.8 79.9 %collective-permute-start.5 = (bf16[512,672]{0,1:T(8,128)(2,1)}, bf16[512,672]{0,1:T(8,128)(2,1)}, u32[]{:S(2)}, u32[]{:S(2)}) collective-permute-start(bf16[512,672]{0,1:T(8,128)(2,1)} %constant_dynamic-slice_fusion.3), channel_id=1, source_target_pairs={{0,8},{4,12},{8,0},{12,4},{1,9},{5,13},{9,1},{13,5},{2,10},{6,14},... | collective-permute-start | bytes 2064392 | tf_op jit(solution)/shard_map/ppermute | solution.py:25
  11.7 100.7 %collective-permute-start.4 = (bf16[512,672]{0,1:T(8,128)(2,1)}, bf16[512,672]{0,1:T(8,128)(2,1)}, u32[]{:S(2)}, u32[]{:S(2)}) collective-permute-start(bf16[512,672]{0,1:T(8,128)(2,1)} %constant_dynamic-slice_fusion.3), channel_id=1, source_target_pairs={{0,16},{16,0},{1,17},{17,1},{2,18},{18,2},{3,19},{19,3},{4,20},{20... | collective-permute-start | bytes 2064392 | tf_op jit(solution)/shard_map/ppermute | solution.py:25
  27.1 47.8 %collective-permute-start.2 = (bf16[768,672]{0,1:T(8,128)(2,1)}, bf16[768,672]{0,1:T(8,128)(2,1)}, u32[]{:S(2)}, u32[]{:S(2)}) collective-permute-start(bf16[768,672]{0,1:T(8,128)(2,1)} %get-tuple-element.23), channel_id=1, source_target_pairs={{0,1},{1,0},{2,3},{3,2},{4,5},{5,4},{6,7},{7,6},{8,9},{9,8},{10,11... | collective-permute-start | bytes 3096584 | tf_op jit(solution)/shard_map/ppermute | solution.py:25
  34.6 66.3 %collective-permute-start = (bf16[512,2,512]{0,2,1:T(8,128)(2,1)}, bf16[512,2,512]{0,2,1:T(8,128)(2,1)}, u32[]{:S(2)}, u32[]{:S(2)}) collective-permute-start(bf16[512,2,512]{0,2,1:T(8,128)(2,1)} %pad_maximum_fusion.12), channel_id=1, source_target_pairs={{0,4},{4,8},{8,12},{1,5},{5,9},{9,13},{2,6},{6,10},{10,14},{3,7},{... | collective-permute-start | bytes 3145736 | tf_op jit(solution)/shard_map/ppermute | solution.py:21
  77.8 48.3 %collective-permute-start.9 = (bf16[768,672]{0,1:T(8,128)(2,1)}, bf16[768,672]{0,1:T(8,128)(2,1)}, u32[]{:S(2)}, u32[]{:S(2)}) collective-permute-start(bf16[768,672]{0,1:T(8,128)(2,1)} %fusion.20), channel_id=1, source_target_pairs={{0,2},{1,3},{2,0},{3,1},{4,6},{5,7},{6,4},{7,5},{8,10},{9,11},{10,... | collective-permute-start | bytes 3096584 | tf_op jit(solution)/shard_map/ppermute | solution.py:25
  88.7 26.4 %collective-permute-start.6 = (bf16[512,672]{0,1:T(8,128)(2,1)}, bf16[512,672]{0,1:T(8,128)(2,1)}, u32[]{:S(2)}, u32[]{:S(2)}) collective-permute-start(bf16[512,672]{0,1:T(8,128)(2,1)} %collective-permute-done.5), channel_id=1, source_target_pairs={{0,16},{16,0},{1,17},{17,1},{2,18},{18,2},{3,19},{19,3},{4,20},{20... | collective-permute-start | bytes 2064392 | tf_op jit(solution)/shard_map/ppermute | solution.py:25
  89.2 46.8 %collective-permute-start.3 = (bf16[768,672]{0,1:T(8,128)(2,1)}, bf16[768,672]{0,1:T(8,128)(2,1)}, u32[]{:S(2)}, u32[]{:S(2)}) collective-permute-start(bf16[768,672]{0,1:T(8,128)(2,1)} %get-tuple-element.14), channel_id=1, source_target_pairs={{0,1},{1,0},{2,3},{3,2},{4,5},{5,4},{6,7},{7,6},{8,9},{9,8},{10,11... | collective-permute-start | bytes 3096584 | tf_op jit(solution)/shard_map/ppermute | solution.py:25
  100.9 39.2 %collective-permute-start.1 = (bf16[512,2,512]{0,2,1:T(8,128)(2,1)}, bf16[512,2,512]{0,2,1:T(8,128)(2,1)}, u32[]{:S(2)}, u32[]{:S(2)}) collective-permute-start(bf16[512,2,512]{0,2,1:T(8,128)(2,1)} %collective-permute-done), channel_id=1, source_target_pairs={{0,4},{4,8},{8,12},{1,5},{5,9},{9,13},{2,6},{6,10},{10,14},{3,7},{... | collective-permute-start | bytes 3145736 | tf_op jit(solution)/shard_map/ppermute | solution.py:21
  129.0 66.7 %collective-permute-start.11 = (bf16[768,672]{0,1:T(8,128)(2,1)}, bf16[768,672]{0,1:T(8,128)(2,1)}, u32[]{:S(2)}, u32[]{:S(2)}) collective-permute-start(bf16[768,672]{0,1:T(8,128)(2,1)} %fusion.22), channel_id=1, source_target_pairs={{0,8},{4,12},{8,0},{12,4},{1,9},{5,13},{9,1},{13,5},{2,10},{6,14},... | collective-permute-start | bytes 3096584 | tf_op jit(solution)/shard_map/ppermute | solution.py:25
  129.0 71.6 %collective-permute-start.10 = (bf16[768,672]{0,1:T(8,128)(2,1)}, bf16[768,672]{0,1:T(8,128)(2,1)}, u32[]{:S(2)}, u32[]{:S(2)}) collective-permute-start(bf16[768,672]{0,1:T(8,128)(2,1)} %fusion.22), channel_id=1, source_target_pairs={{0,16},{16,0},{1,17},{17,1},{2,18},{18,2},{3,19},{19,3},{4,20},{20... | collective-permute-start | bytes 3096584 | tf_op jit(solution)/shard_map/ppermute | solution.py:25
  137.3 48.5 %collective-permute-start.7 = (bf16[640,672]{0,1:T(8,128)(2,1)}, bf16[640,672]{0,1:T(8,128)(2,1)}, u32[]{:S(2)}, u32[]{:S(2)}) collective-permute-start(bf16[640,672]{0,1:T(8,128)(2,1)} %copy.88), channel_id=1, source_target_pairs={{0,1},{1,0},{2,3},{3,2},{4,5},{5,4},{6,7},{7,6},{8,9},{9,8},{10,11... | collective-permute-start | bytes 2580488 | tf_op jit(solution)/shard_map/ppermute | solution.py:25
  140.1 57.1 %collective-permute-start.13 = (bf16[768,672]{0,1:T(8,128)(2,1)}, bf16[768,672]{0,1:T(8,128)(2,1)}, u32[]{:S(2)}, u32[]{:S(2)}) collective-permute-start(bf16[768,672]{0,1:T(8,128)(2,1)} %fusion.18), channel_id=1, source_target_pairs={{0,2},{1,3},{2,0},{3,1},{4,6},{5,7},{6,4},{7,5},{8,10},{9,11},{10,... | collective-permute-start | bytes 3096584 | tf_op jit(solution)/shard_map/ppermute | solution.py:25
  185.8 25.8 %collective-permute-start.8 = (bf16[512,672]{0,1:T(8,128)(2,1)}, bf16[512,672]{0,1:T(8,128)(2,1)}, u32[]{:S(2)}, u32[]{:S(2)}) collective-permute-start(bf16[512,672]{0,1:T(8,128)(2,1)} %fusion.41), channel_id=1, source_target_pairs={{0,1},{1,0},{2,3},{3,2},{4,5},{5,4},{6,7},{7,6},{8,9},{9,8},{10,11... | collective-permute-start | bytes 2064392 | tf_op jit(solution)/shard_map/ppermute | solution.py:25
  192.9 38.9 %collective-permute-start.15 = (bf16[640,672]{0,1:T(8,128)(2,1)}, bf16[640,672]{0,1:T(8,128)(2,1)S(1)}, u32[]{:S(2)}, u32[]{:S(2)}) collective-permute-start(bf16[640,672]{0,1:T(8,128)(2,1)} %copy.90), channel_id=1, source_target_pairs={{0,2},{1,3},{2,0},{3,1},{4,6},{5,7},{6,4},{7,5},{8,10},{9,11},{10,... | collective-permute-start | bytes 2580488 | tf_op jit(solution)/shard_map/ppermute | solution.py:25
  195.7 42.0 %collective-permute-start.12 = (bf16[768,672]{0,1:T(8,128)(2,1)}, bf16[768,672]{0,1:T(8,128)(2,1)}, u32[]{:S(2)}, u32[]{:S(2)}) collective-permute-start(bf16[768,672]{0,1:T(8,128)(2,1)} %collective-permute-done.11), channel_id=1, source_target_pairs={{0,16},{16,0},{1,17},{17,1},{2,18},{18,2},{3,19},{19,3},{4,20},{20... | collective-permute-start | bytes 3096584 | tf_op jit(solution)/shard_map/ppermute | solution.py:25
  200.1 43.8 %collective-permute-start.14 = (bf16[768,672]{0,1:T(8,128)(2,1)}, bf16[768,672]{0,1:T(8,128)(2,1)}, u32[]{:S(2)}, u32[]{:S(2)}) collective-permute-start(bf16[768,672]{0,1:T(8,128)(2,1)} %fusion.24), channel_id=1, source_target_pairs={{0,16},{16,0},{1,17},{17,1},{2,18},{18,2},{3,19},{19,3},{4,20},{20... | collective-permute-start | bytes 3096584 | tf_op jit(solution)/shard_map/ppermute | solution.py:25
  200.6 54.3 %collective-permute-start.24 = (bf16[768,672]{0,1:T(8,128)(2,1)}, bf16[768,672]{0,1:T(8,128)(2,1)}, u32[]{:S(2)}, u32[]{:S(2)}) collective-permute-start(bf16[768,672]{0,1:T(8,128)(2,1)} %fusion.24), channel_id=1, source_target_pairs={{0,8},{4,12},{8,0},{12,4},{1,9},{5,13},{9,1},{13,5},{2,10},{6,14},... | collective-permute-start | bytes 3096584 | tf_op jit(solution)/shard_map/ppermute | solution.py:25
  236.2 38.3 %collective-permute-start.16 = (bf16[640,672]{0,1:T(8,128)(2,1)S(1)}, bf16[640,672]{0,1:T(8,128)(2,1)S(1)}, u32[]{:S(2)}, u32[]{:S(2)}) collective-permute-start(bf16[640,672]{0,1:T(8,128)(2,1)S(1)} %copy.92), channel_id=1, source_target_pairs={{0,16},{16,0},{1,17},{17,1},{2,18},{18,2},{3,19},{19,3},{4,20},{20... | collective-permute-start | bytes 2580488 | tf_op jit(solution)/shard_map/ppermute | solution.py:25
  240.7 29.8 %collective-permute-start.17 = (bf16[512,672]{0,1:T(8,128)(2,1)S(1)}, bf16[512,672]{0,1:T(8,128)(2,1)S(1)}, u32[]{:S(2)}, u32[]{:S(2)}) collective-permute-start(bf16[512,672]{0,1:T(8,128)(2,1)S(1)} %copy-done.10), channel_id=1, source_target_pairs={{0,2},{1,3},{2,0},{3,1},{4,6},{5,7},{6,4},{7,5},{8,10},{9,11},{10,... | collective-permute-start | bytes 2064392 | tf_op jit(solution)/shard_map/ppermute | solution.py:25
  240.8 58.8 %collective-permute-start.20 = (bf16[1536,672]{0,1:T(8,128)(2,1)}, bf16[1536,672]{0,1:T(8,128)(2,1)}, u32[]{:S(2)}, u32[]{:S(2)}) collective-permute-start(bf16[1536,672]{0,1:T(8,128)(2,1)} %pad_maximum_fusion.2), channel_id=1, source_target_pairs={{0,4},{4,0},{8,12},{12,8},{1,5},{5,1},{9,13},{13,9},{2,6},{6,2},{1... | collective-permute-start | bytes 6193160 | tf_op jit(solution)/shard_map/ppermute | solution.py:25
  246.9 57.5 %collective-permute-start.21 = (bf16[1536,672]{0,1:T(8,128)(2,1)}, bf16[1536,672]{0,1:T(8,128)(2,1)}, u32[]{:S(2)}, u32[]{:S(2)}) collective-permute-start(bf16[1536,672]{0,1:T(8,128)(2,1)} %pad_maximum_fusion.4), channel_id=1, source_target_pairs={{0,4},{4,0},{8,12},{12,8},{1,5},{5,1},{9,13},{13,9},{2,6},{6,2},{1... | collective-permute-start | bytes 6193160 | tf_op jit(solution)/shard_map/ppermute | solution.py:25
  254.9 30.2 %collective-permute-start.25 = (bf16[768,672]{0,1:T(8,128)(2,1)}, bf16[768,672]{0,1:T(8,128)(2,1)}, u32[]{:S(2)}, u32[]{:S(2)}) collective-permute-start(bf16[768,672]{0,1:T(8,128)(2,1)} %collective-permute-done.24), channel_id=1, source_target_pairs={{0,16},{16,0},{1,17},{17,1},{2,18},{18,2},{3,19},{19,3},{4,20},{20... | collective-permute-start | bytes 3096584 | tf_op jit(solution)/shard_map/ppermute | solution.py:25
  275.5 35.1 %collective-permute-start.29 = (bf16[1536,672]{0,1:T(8,128)(2,1)}, bf16[1536,672]{0,1:T(8,128)(2,1)}, u32[]{:S(2)}, u32[]{:S(2)}) collective-permute-start(bf16[1536,672]{0,1:T(8,128)(2,1)} %pad_maximum_fusion.3), channel_id=1, source_target_pairs={{0,4},{4,0},{8,12},{12,8},{1,5},{5,1},{9,13},{13,9},{2,6},{6,2},{1... | collective-permute-start | bytes 6193160 | tf_op jit(solution)/shard_map/ppermute | solution.py:25
  285.1 24.3 %collective-permute-start.19 = (bf16[1024,672]{0,1:T(8,128)(2,1)S(1)}, bf16[1024,672]{0,1:T(8,128)(2,1)S(1)}, u32[]{:S(2)}, u32[]{:S(2)}) collective-permute-start(bf16[1024,672]{0,1:T(8,128)(2,1)S(1)} %copy-done.2), channel_id=1, source_target_pairs={{0,4},{4,0},{8,12},{12,8},{1,5},{5,1},{9,13},{13,9},{2,6},{6,2},{1... | collective-permute-start | bytes 4128776 | tf_op jit(solution)/shard_map/ppermute | solution.py:25
  295.9 40.7 %collective-permute-start.26 = (bf16[1280,672]{0,1:T(8,128)(2,1)}, bf16[1280,672]{0,1:T(8,128)(2,1)S(1)}, u32[]{:S(2)}, u32[]{:S(2)}) collective-permute-start(bf16[1280,672]{0,1:T(8,128)(2,1)} %copy.94), channel_id=1, source_target_pairs={{0,8},{4,12},{8,0},{12,4},{1,9},{5,13},{9,1},{13,5},{2,10},{6,14},... | collective-permute-start | bytes 5160968 | tf_op jit(solution)/shard_map/ppermute | solution.py:25
  299.9 37.7 %collective-permute-start.22 = (bf16[1280,672]{0,1:T(8,128)(2,1)S(1)}, bf16[1280,672]{0,1:T(8,128)(2,1)S(1)}, u32[]{:S(2)}, u32[]{:S(2)}) collective-permute-start(bf16[1280,672]{0,1:T(8,128)(2,1)S(1)} %copy-done.12), channel_id=1, source_target_pairs={{0,4},{4,0},{8,12},{12,8},{1,5},{5,1},{9,13},{13,9},{2,6},{6,2},{1... | collective-permute-start | bytes 5160968 | tf_op jit(solution)/shard_map/ppermute | solution.py:25
  304.5 60.0 %collective-permute-start.27 = (bf16[1024,672]{0,1:T(8,128)(2,1)S(1)}, bf16[1024,672]{0,1:T(8,128)(2,1)S(1)}, u32[]{:S(2)}, u32[]{:S(2)}) collective-permute-start(bf16[1024,672]{0,1:T(8,128)(2,1)S(1)} %pad_maximum_fusion.10), channel_id=1, source_target_pairs={{0,8},{4,12},{8,0},{12,4},{1,9},{5,13},{9,1},{13,5},{2,10},{6,14},... | collective-permute-start | bytes 4128776 | tf_op jit(solution)/shard_map/ppermute | solution.py:25
  309.4 59.5 %collective-permute-start.28 = (bf16[1024,672]{0,1:T(8,128)(2,1)S(1)}, bf16[1024,672]{0,1:T(8,128)(2,1)S(1)}, u32[]{:S(2)}, u32[]{:S(2)}) collective-permute-start(bf16[1024,672]{0,1:T(8,128)(2,1)S(1)} %copy-done.14), channel_id=1, source_target_pairs={{0,4},{4,0},{8,12},{12,8},{1,5},{5,1},{9,13},{13,9},{2,6},{6,2},{1... | collective-permute-start | bytes 4128776 | tf_op jit(solution)/shard_map/ppermute | solution.py:25
  310.9 56.7 %collective-permute-start.30 = (bf16[1536,672]{0,1:T(8,128)(2,1)S(1)}, bf16[1536,672]{0,1:T(8,128)(2,1)S(1)}, u32[]{:S(2)}, u32[]{:S(2)}) collective-permute-start(bf16[1536,672]{0,1:T(8,128)(2,1)S(1)} %copy-done.34), channel_id=1, source_target_pairs={{0,4},{4,0},{8,12},{12,8},{1,5},{5,1},{9,13},{13,9},{2,6},{6,2},{1... | collective-permute-start | bytes 6193160 | tf_op jit(solution)/shard_map/ppermute | solution.py:25
  336.6 30.2 %collective-permute-start.23 = (bf16[1024,672]{0,1:T(8,128)(2,1)S(1)}, bf16[1024,672]{0,1:T(8,128)(2,1)S(1)}, u32[]{:S(2)}, u32[]{:S(2)}) collective-permute-start(bf16[1024,672]{0,1:T(8,128)(2,1)S(1)} %pad_maximum_fusion.10), channel_id=1, source_target_pairs={{0,4},{4,0},{8,12},{12,8},{1,5},{5,1},{9,13},{13,9},{2,6},{6,2},{1... | collective-permute-start | bytes 4128776 | tf_op jit(solution)/shard_map/ppermute | solution.py:25
  337.7 32.2 %collective-permute-start.31 = (bf16[1280,672]{0,1:T(8,128)(2,1)S(1)}, bf16[1280,672]{0,1:T(8,128)(2,1)S(1)}, u32[]{:S(2)}, u32[]{:S(2)}) collective-permute-start(bf16[1280,672]{0,1:T(8,128)(2,1)S(1)} %collective-permute-done.26), channel_id=1, source_target_pairs={{0,4},{4,0},{8,12},{12,8},{1,5},{5,1},{9,13},{13,9},{2,6},{6,2},{1... | collective-permute-start | bytes 5160968 | tf_op jit(solution)/shard_map/ppermute | solution.py:25
  (39 other events, 339.2 us)
Sparse Core Ops, SparseCore 0:
  378.9 51.5 reduce-scatter.3

commit v4 on v3

--- a/solution.py
+++ b/solution.py
@@ -196,7 +196,7 @@
                 high_side == 0, own_values + other_values, other_values - own_values
             ).astype(jnp.bfloat16)
         lefts.append(own_and_other(rotated, group_index, begin, rows, half))
-        wides.append(over_chips(piece, chunk < 2))
+        wides.append(over_chips(piece, True))
     totals = {
         distance: jnp.dot(tokens_left, columns, preferred_element_type=jnp.float32)
         for distance, columns in spread(out_wide, [0]).items()

time: 443 us -> 425 us (0.959)
  waiting for transfers between devices: 162 us -> 189 us
  local copies, waits for them, and re-layouts: 58.1 us -> 35.8 us
  matrix products: 103 us -> 88.1 us
  other arithmetic: 70.9 us -> 59.9 us
    ppermute x31 -> x33, waiting for transfers between devices: 110 us -> 138 us  [swapped(): lax.ppermute(x, axis, [(i, i ^ 1 << stride) for i in range(lax.axis_size(...]
    dot_general x16, matrix products: 33.3 us -> 17.8 us  [per_device(): jnp.dot(left, columns, preferred_element_type=jnp.float32)]
    concatenate x7, other arithmetic: 17.2 us -> 8.58 us  [both_groups(): return jnp.concatenate([piece, swapped(piece, 'group', 0)], axis=0)]
    unnamed x80 -> x55, local copies, waits for them, and re-layouts: 21.2 us -> 15.1 us
    concatenate x2 -> x3, local copies, waits for them, and re-layouts: 6.32 us -> 0.27 us  [both_groups(): return jnp.concatenate([piece, swapped(piece, 'group', 0)], axis=0)]
    ppermute x3 -> x0, local copies, waits for them, and re-layouts: 5.47 us -> none  [swapped(): lax.ppermute(x, axis, [(i, i ^ 1 << stride) for i in range(lax.axis_size(...]
    convert_element_type x8, other arithmetic: 18.1 us -> 12.8 us  [per_device(): piece = jnp.where(high_side == 0, own_values + other_values, other_values...]
    ppermute x31 -> x33, starting transfers between devices: 24.4 us -> 26.7 us  [swapped(): lax.ppermute(x, axis, [(i, i ^ 1 << stride) for i in range(lax.axis_size(...]
  transfers between devices with their start and end apart: 34 -> 36, of which waited for: 10 -> 15; matrix products, arithmetic and copies ran while one was open for 50% -> 41% of each run, Pallas kernels for 0% -> 0%
where the time goes in v4:
time: 425 us; the launch traced here: 420 us
  waiting for transfers between devices  189 us (44%)
  matrix products  88.1 us (21%)
  other arithmetic  59.9 us (14%)
  local copies, waits for them, and re-layouts  35.8 us (8%)
  starting transfers between devices  31.7 us (7%)
  between operations  15 us (4%)
    ppermute x33, waiting for transfers between devices, swapped(): lax.ppermute(x, axis, [(i, i ^ 1 << stride) for i in range(lax.axis_size(...  138 us
    reduce_scatter x1, waiting for transfers between devices, per_device(): return lax.psum_scatter(partials, 'tp', scatter_dimension=0, tiled=True)  51.6 us
    dot_general x2, matrix products, per_device(): jnp.dot(hidden[:, first:first + width], mixer, preferred_element_type=jnp...  27.8 us
    ppermute x33, starting transfers between devices, swapped(): lax.ppermute(x, axis, [(i, i ^ 1 << stride) for i in range(lax.axis_size(...  26.7 us
    dot_general x16, matrix products, per_device(): jnp.dot(left, columns, preferred_element_type=jnp.float32)  17.8 us
    unnamed x55, local copies, waits for them, and re-layouts  15.1 us
    dot_general x1, matrix products, per_device(): jnp.einsum('kgqs,skd->qkgd', weights_soft, value_rows, preferred_element_...  14.1 us
    convert_element_type x8, other arithmetic, per_device(): piece = jnp.where(high_side == 0, own_values + other_values, other_values...  12.8 us
  transfers between devices with their start and end apart: 36, of which 15 were waited for; matrix products, arithmetic and copies ran while one was open for 41% of the time, Pallas kernels for 0%

profile of v4, /device:TPU:0, one launch (start us, length us, event | category | flops | bytes accessed | tf_op | source)
XLA Modules:
  0.0 420.0 jit_solution(1769543208547368721)
XLA Ops:
  8.8 3.0 collective-permute-start.5
  19.3 3.0 copy.85
  22.3 4.9 %multiply_convert_fusion.2 = (bf16[768,672]{0,1:T(8,128)(2,1)}, bf16[768,672]{0,1:T(8,128)(2,1)}) fusion(s32[768,672]{0,1:T(8,128)} %copy.85, s32[5376,672]{0,1:T(8,128)} %param.14, s32[]{:T(128)S(6)} %select_n.171, s32[768,672]{0,1:T(8,128)S(1)} %copy.84, s32[]{:T(128)S(6)} %select_n.168), kind=kLoop, calls=%fused_computation.71 | loop fusion | flops 5160960 | bytes 10321928 | tf_op jit(solution)/shard_map/convert_element_type | solution.py:180
  34.6 2.8 collective-permute-start
  40.1 11.8 %fusion.11 = f32[2688,512]{1,0:T(8,128)S(1)} fusion(bf16[2688,2688]{1,0:T(8,128)(2,1)} %constant.159.clone, bf16[512,5376]{1,0:T(8,128)(2,1)} %param.13), kind=kOutput, calls=%fused_computation.39 | convolution fusion | flops 7398752256 | bytes 22708224 | tf_op jit(solution)/shard_map/dot_general | solution.py:147
  51.9 16.0 %fusion.10 = (bf16[512,2688]{0,1:T(8,128)(2,1)}, bf16[512,2688]{0,1:T(8,128)(2,1)}) fusion(f32[2688,512]{1,0:T(8,128)S(1)} %fusion.11, bf16[2688,2688]{1,0:T(8,128)(2,1)} %constant.159.clone, bf16[512,5376]{1,0:T(8,128)(2,1)} %param.13), kind=kOutput, calls=%fused_computation.36 | convolution fusion | flops 7407009792 | bytes 28213248 | tf_op jit(solution)/shard_map/dot_general | solution.py:147
  73.7 3.8 subtract_convert_fusion
  79.9 2.9 fusion.20
  89.7 5.7 %fusion.39 = (bf16[512,768]{0,1:T(8,128)(2,1)}, bf16[512,768]{0,1:T(8,128)(2,1)}, bf16[512,768]{0,1:T(8,128)(2,1)}, bf16[512,768]{0,1:T(8,128)(2,1)}) fusion(s32[]{:T(128)S(6)} %select_n.171, bf16[512,2688]{0,1:T(8,128)(2,1)} %get-tuple-element.26, bf16[512,2688]{0,1:T(8,128)(2,1)} %get-tuple-element.25, s32[]{:T(128)S(6)} %select_n.175, s32[]{:T(128)S(6)} %select_n.168, ...), kind=kLoop, calls=%fused_computation.110 | loop fusion | flops 6291456 | bytes 8650768 | tf_op jit(solution)/shard_map/concatenate | solution.py:157
  95.3 4.7 %copy.76 = bf16[1024,2,512]{0,2,1:T(8,128)(2,1)} copy(bf16[1024,2,512]{2,1,0:T(2,128)(2,1)S(1)} %copy-done.13) | data formatting | bytes 4194304 | tf_op args[2]
  100.5 3.6 fusion.16
  106.4 3.3 fusion.50
  109.7 3.3 fusion.47
  118.1 13.1 %collective-permute-done.9 = bf16[768,672]{0,1:T(8,128)(2,1)} collective-permute-done((bf16[768,672]{0,1:T(8,128)(2,1)}, bf16[768,672]{0,1:T(8,128)(2,1)}, u32[]{:S(2)}, u32[]{:S(2)}) %collective-permute-start.9) | collective-permute-done | bytes 1032224 | tf_op jit(solution)/shard_map/ppermute | solution.py:25
  131.2 2.9 fusion.22
  134.6 12.1 %collective-permute-done.3 = bf16[768,672]{0,1:T(8,128)(2,1)} collective-permute-done((bf16[768,672]{0,1:T(8,128)(2,1)S(1)}, bf16[768,672]{0,1:T(8,128)(2,1)}, u32[]{:S(2)}, u32[]{:S(2)}) %collective-permute-start.3) | collective-permute-done | bytes 1032224 | tf_op jit(solution)/shard_map/ppermute | solution.py:25
  149.3 2.8 fusion.15
  154.5 12.0 %fusion.51 = f32[4,1536,512,2]{2,1,3,0:T(8,128)} fusion(bf16[1536,4,128,1]{0,2,3,1:T(8,128)(2,1)S(1)} %bitcast.99, bf16[512,4,2,64]{3,0,2,1:T(8,128)(2,1)S(1)} %bitcast.107, bf16[512,4,2,64]{3,0,2,1:T(8,128)(2,1)S(1)} %bitcast.104), kind=kOutput, calls=%fused_computation.132 | convolution fusion | flops 1612709888 | bytes 27787264 | tf_op jit(solution)/shard_map/qkgd,skd->kgqs/dot_general | solution.py:127
  166.5 10.2 %fusion.82 = f32[4,2,512]{2,1,0:T(2,128)S(1)} fusion(pred[512,1536]{0,1:T(8,128)(4,1)} %fusion.8, bf16[1536,4,128,1]{0,2,3,1:T(8,128)(2,1)S(1)} %bitcast.100, bf16[512,4,2,64]{3,0,2,1:T(8,128)(2,1)} %bitcast.106, bf16[512,4,2,64]{3,0,2,1:T(8,128)(2,1)S(1)} %bitcast.105), kind=kOutput, calls=%fused_computation.176 | convolution fusion | flops 1637877248 | bytes 3424256 | tf_op jit(solution)/shard_map/sub | solution.py:135
  176.7 14.1 %fusion.29 = bf16[4,128,2,512]{3,1,2,0:T(8,128)(2,1)S(1)} fusion(bf16[1536,4,128,1]{0,2,3,1:T(8,128)(2,1)} %bitcast.109, f32[4,2,512]{2,1,0:T(2,128)S(1)} %fusion.82, f32[4,1536,512,2]{2,1,3,0:T(8,128)} %fusion.51, pred[512,1536]{0,1:T(8,128)(4,1)} %fusion.8), kind=kOutput, calls=%fused_computation.85 | convolution fusion | flops 1642599936 | bytes 28590080 | tf_op jit(solution)/shard_map/kgqs,skd->qkgd/dot_general | solution.py:139
  196.9 2.8 collective-permute-start.15
  205.5 18.5 %collective-permute-done.8 = bf16[512,672]{0,1:T(8,128)(2,1)S(1)} collective-permute-done((bf16[512,672]{0,1:T(8,128)(2,1)S(1)}, bf16[512,672]{0,1:T(8,128)(2,1)S(1)}, u32[]{:S(2)}, u32[]{:S(2)}) %collective-permute-start.8) | collective-permute-done | bytes 688160 | tf_op jit(solution)/shard_map/ppermute | solution.py:25
  224.2 13.6 %collective-permute-done.15 = bf16[640,672]{0,1:T(8,128)(2,1)S(1)} collective-permute-done((bf16[640,672]{0,1:T(8,128)(2,1)S(1)}, bf16[640,672]{0,1:T(8,128)(2,1)S(1)}, u32[]{:S(2)}, u32[]{:S(2)}) %collective-permute-start.15) | collective-permute-done | bytes 860192 | tf_op jit(solution)/shard_map/ppermute | solution.py:25
  241.1 6.7 %collective-permute-done.14 = bf16[768,672]{0,1:T(8,128)(2,1)S(1)} collective-permute-done((bf16[768,672]{0,1:T(8,128)(2,1)S(1)}, bf16[768,672]{0,1:T(8,128)(2,1)S(1)}, u32[]{:S(2)}, u32[]{:S(2)}) %collective-permute-start.14) | collective-permute-done | bytes 1032224 | tf_op jit(solution)/shard_map/ppermute | solution.py:25
  255.0 11.2 %collective-permute-done.16 = bf16[640,672]{0,1:T(8,128)(2,1)S(1)} collective-permute-done((bf16[640,672]{0,1:T(8,128)(2,1)S(1)}, bf16[640,672]{0,1:T(8,128)(2,1)S(1)}, u32[]{:S(2)}, u32[]{:S(2)}) %collective-permute-start.16) | collective-permute-done | bytes 860192 | tf_op jit(solution)/shard_map/ppermute | solution.py:25
  269.7 9.2 %collective-permute-done.17 = bf16[512,672]{0,1:T(8,128)(2,1)S(1)} collective-permute-done((bf16[512,672]{0,1:T(8,128)(2,1)S(1)}, bf16[512,672]{0,1:T(8,128)(2,1)S(1)}, u32[]{:S(2)}, u32[]{:S(2)}) %collective-permute-start.17) | collective-permute-done | bytes 688160 | tf_op jit(solution)/shard_map/ppermute | solution.py:25
  280.7 7.6 %collective-permute-done.25 = bf16[768,672]{0,1:T(8,128)(2,1)S(1)} collective-permute-done((bf16[768,672]{0,1:T(8,128)(2,1)S(1)}, bf16[768,672]{0,1:T(8,128)(2,1)S(1)}, u32[]{:S(2)}, u32[]{:S(2)}) %collective-permute-start.25) | collective-permute-done | bytes 1032224 | tf_op jit(solution)/shard_map/ppermute | solution.py:25
  289.7 17.1 %collective-permute-done.27 = bf16[640,672]{0,1:T(8,128)(2,1)S(1)} collective-permute-done((bf16[640,672]{0,1:T(8,128)(2,1)S(1)}, bf16[640,672]{0,1:T(8,128)(2,1)S(1)}, u32[]{:S(2)}, u32[]{:S(2)}) %collective-permute-start.27) | collective-permute-done | bytes 860192 | tf_op jit(solution)/shard_map/ppermute | solution.py:25
  308.0 12.5 %collective-permute-done.18 = bf16[512,672]{0,1:T(8,128)(2,1)S(1)} collective-permute-done((bf16[512,672]{0,1:T(8,128)(2,1)S(1)}, bf16[512,672]{0,1:T(8,128)(2,1)S(1)}, u32[]{:S(2)}, u32[]{:S(2)}) %collective-permute-start.18) | collective-permute-done | bytes 688160 | tf_op jit(solution)/shard_map/ppermute | solution.py:25
  325.6 13.1 %collective-permute-done.29 = bf16[512,672]{0,1:T(8,128)(2,1)S(1)} collective-permute-done((bf16[512,672]{0,1:T(8,128)(2,1)S(1)}, bf16[512,672]{0,1:T(8,128)(2,1)S(1)}, u32[]{:S(2)}, u32[]{:S(2)}) %collective-permute-start.29) | collective-permute-done | bytes 688160 | tf_op jit(solution)/shard_map/ppermute | solution.py:25
  356.7 4.6 %copy.94 = bf16[512,2688]{1,0:T(8,128)(2,1)} copy(bf16[512,2688]{0,1:T(8,128)(2,1)} %pad_maximum_fusion.1) | data formatting | bytes 5505024
  361.4 51.6 %reduce-scatter.4.cloned.1.call-done = bf16[128,2688]{1,0:T(8,128)(2,1)} async-done(((bf16[512,2688]{1,0:T(8,128)(2,1)}), bf16[128,2688]{1,0:T(8,128)(2,1)}) %reduce-scatter.4.cloned.1.call-update) | async-done | bytes 688144 | tf_op jit(solution)/shard_map/reduce_scatter | solution.py:215
  (181 shorter events, 100.6 us)
Async XLA Ops:
  6.5 406.4 %reduce-scatter.4.cloned.1.call-start = ((), (), s32[]{:S(2)}) async-start(), calls=%async_computation.1 | async-start | bytes 3440640 | tf_op jit(solution)/shard_map/reduce_scatter | solution.py:215
  8.8 80.3 %collective-permute-start.5 = (bf16[512,672]{0,1:T(8,128)(2,1)}, bf16[512,672]{0,1:T(8,128)(2,1)}, u32[]{:S(2)}, u32[]{:S(2)}) collective-permute-start(bf16[512,672]{0,1:T(8,128)(2,1)} %constant_dynamic-slice_fusion.2), channel_id=1, source_target_pairs={{0,8},{4,12},{8,0},{12,4},{1,9},{5,13},{9,1},{13,5},{2,10},{6,14},... | collective-permute-start | bytes 2064392 | tf_op jit(solution)/shard_map/ppermute | solution.py:25
  11.7 101.3 %collective-permute-start.4 = (bf16[512,672]{0,1:T(8,128)(2,1)}, bf16[512,672]{0,1:T(8,128)(2,1)}, u32[]{:S(2)}, u32[]{:S(2)}) collective-permute-start(bf16[512,672]{0,1:T(8,128)(2,1)} %constant_dynamic-slice_fusion.2), channel_id=1, source_target_pairs={{0,16},{16,0},{1,17},{17,1},{2,18},{18,2},{3,19},{19,3},{4,20},{20... | collective-permute-start | bytes 2064392 | tf_op jit(solution)/shard_map/ppermute | solution.py:25
  27.2 52.7 %collective-permute-start.2 = (bf16[768,672]{0,1:T(8,128)(2,1)}, bf16[768,672]{0,1:T(8,128)(2,1)}, u32[]{:S(2)}, u32[]{:S(2)}) collective-permute-start(bf16[768,672]{0,1:T(8,128)(2,1)} %get-tuple-element.23), channel_id=1, source_target_pairs={{0,1},{1,0},{2,3},{3,2},{4,5},{5,4},{6,7},{7,6},{8,9},{9,8},{10,11... | collective-permute-start | bytes 3096584 | tf_op jit(solution)/shard_map/ppermute | solution.py:25
  34.6 69.4 %collective-permute-start = (bf16[512,2,512]{0,2,1:T(8,128)(2,1)}, bf16[512,2,512]{0,2,1:T(8,128)(2,1)}, u32[]{:S(2)}, u32[]{:S(2)}) collective-permute-start(bf16[512,2,512]{0,2,1:T(8,128)(2,1)} %pad_maximum_fusion.12), channel_id=1, source_target_pairs={{0,4},{4,8},{8,12},{1,5},{5,9},{9,13},{2,6},{6,10},{10,14},{3,7},{... | collective-permute-start | bytes 3145736 | tf_op jit(solution)/shard_map/ppermute | solution.py:21
  82.8 48.3 %collective-permute-start.9 = (bf16[768,672]{0,1:T(8,128)(2,1)}, bf16[768,672]{0,1:T(8,128)(2,1)}, u32[]{:S(2)}, u32[]{:S(2)}) collective-permute-start(bf16[768,672]{0,1:T(8,128)(2,1)} %fusion.20), channel_id=1, source_target_pairs={{0,2},{1,3},{2,0},{3,1},{4,6},{5,7},{6,4},{7,5},{8,10},{9,11},{10,... | collective-permute-start | bytes 3096584 | tf_op jit(solution)/shard_map/ppermute | solution.py:25
  89.1 26.4 %collective-permute-start.6 = (bf16[512,672]{0,1:T(8,128)(2,1)}, bf16[512,672]{0,1:T(8,128)(2,1)}, u32[]{:S(2)}, u32[]{:S(2)}) collective-permute-start(bf16[512,672]{0,1:T(8,128)(2,1)} %collective-permute-done.5), channel_id=1, source_target_pairs={{0,16},{16,0},{1,17},{17,1},{2,18},{18,2},{3,19},{19,3},{4,20},{20... | collective-permute-start | bytes 2064392 | tf_op jit(solution)/shard_map/ppermute | solution.py:25
  100.0 46.6 %collective-permute-start.3 = (bf16[768,672]{0,1:T(8,128)(2,1)S(1)}, bf16[768,672]{0,1:T(8,128)(2,1)}, u32[]{:S(2)}, u32[]{:S(2)}) collective-permute-start(bf16[768,672]{0,1:T(8,128)(2,1)S(1)} %copy-done.11), channel_id=1, source_target_pairs={{0,1},{1,0},{2,3},{3,2},{4,5},{5,4},{6,7},{7,6},{8,9},{9,8},{10,11... | collective-permute-start | bytes 3096584 | tf_op jit(solution)/shard_map/ppermute | solution.py:25
  104.1 45.1 %collective-permute-start.1 = (bf16[512,2,512]{0,2,1:T(8,128)(2,1)}, bf16[512,2,512]{0,2,1:T(8,128)(2,1)}, u32[]{:S(2)}, u32[]{:S(2)}) collective-permute-start(bf16[512,2,512]{0,2,1:T(8,128)(2,1)} %collective-permute-done), channel_id=1, source_target_pairs={{0,4},{4,8},{8,12},{1,5},{5,9},{9,13},{2,6},{6,10},{10,14},{3,7},{... | collective-permute-start | bytes 3145736 | tf_op jit(solution)/shard_map/ppermute | solution.py:21
  134.1 62.9 %collective-permute-start.11 = (bf16[768,672]{0,1:T(8,128)(2,1)}, bf16[768,672]{0,1:T(8,128)(2,1)}, u32[]{:S(2)}, u32[]{:S(2)}) collective-permute-start(bf16[768,672]{0,1:T(8,128)(2,1)} %fusion.22), channel_id=1, source_target_pairs={{0,8},{4,12},{8,0},{12,4},{1,9},{5,13},{9,1},{13,5},{2,10},{6,14},... | collective-permute-start | bytes 3096584 | tf_op jit(solution)/shard_map/ppermute | solution.py:25
  134.1 69.1 %collective-permute-start.10 = (bf16[768,672]{0,1:T(8,128)(2,1)}, bf16[768,672]{0,1:T(8,128)(2,1)}, u32[]{:S(2)}, u32[]{:S(2)}) collective-permute-start(bf16[768,672]{0,1:T(8,128)(2,1)} %fusion.22), channel_id=1, source_target_pairs={{0,16},{16,0},{1,17},{17,1},{2,18},{18,2},{3,19},{19,3},{4,20},{20... | collective-permute-start | bytes 3096584 | tf_op jit(solution)/shard_map/ppermute | solution.py:25
  146.6 46.3 %collective-permute-start.7 = (bf16[640,672]{0,1:T(8,128)(2,1)}, bf16[640,672]{0,1:T(8,128)(2,1)}, u32[]{:S(2)}, u32[]{:S(2)}) collective-permute-start(bf16[640,672]{0,1:T(8,128)(2,1)} %multiply_convert_fusion.4), channel_id=1, source_target_pairs={{0,1},{1,0},{2,3},{3,2},{4,5},{5,4},{6,7},{7,6},{8,9},{9,8},{10,11... | collective-permute-start | bytes 2580488 | tf_op jit(solution)/shard_map/ppermute | solution.py:25
  149.2 50.6 %collective-permute-start.13 = (bf16[768,672]{0,1:T(8,128)(2,1)}, bf16[768,672]{0,1:T(8,128)(2,1)}, u32[]{:S(2)}, u32[]{:S(2)}) collective-permute-start(bf16[768,672]{0,1:T(8,128)(2,1)} %fusion.18), channel_id=1, source_target_pairs={{0,2},{1,3},{2,0},{3,1},{4,6},{5,7},{6,4},{7,5},{8,10},{9,11},{10,... | collective-permute-start | bytes 3096584 | tf_op jit(solution)/shard_map/ppermute | solution.py:25
  149.2 190.5 %collective-permute-start.19 = (bf16[1024,672]{0,1:T(8,128)(2,1)}, bf16[1024,672]{0,1:T(8,128)(2,1)}, u32[]{:S(2)}, u32[]{:S(2)}) collective-permute-start(bf16[1024,672]{0,1:T(8,128)(2,1)} %pad_maximum_fusion.8), channel_id=1, source_target_pairs={{0,4},{4,0},{8,12},{12,8},{1,5},{5,1},{9,13},{13,9},{2,6},{6,2},{1... | collective-permute-start | bytes 4128776 | tf_op jit(solution)/shard_map/ppermute | solution.py:25
  193.2 30.8 %collective-permute-start.8 = (bf16[512,672]{0,1:T(8,128)(2,1)S(1)}, bf16[512,672]{0,1:T(8,128)(2,1)S(1)}, u32[]{:S(2)}, u32[]{:S(2)}) collective-permute-start(bf16[512,672]{0,1:T(8,128)(2,1)S(1)} %copy-done.12), channel_id=1, source_target_pairs={{0,1},{1,0},{2,3},{3,2},{4,5},{5,4},{6,7},{7,6},{8,9},{9,8},{10,11... | collective-permute-start | bytes 2064392 | tf_op jit(solution)/shard_map/ppermute | solution.py:25
  196.9 40.8 %collective-permute-start.15 = (bf16[640,672]{0,1:T(8,128)(2,1)S(1)}, bf16[640,672]{0,1:T(8,128)(2,1)S(1)}, u32[]{:S(2)}, u32[]{:S(2)}) collective-permute-start(bf16[640,672]{0,1:T(8,128)(2,1)S(1)} %fusion.26), channel_id=1, source_target_pairs={{0,2},{1,3},{2,0},{3,1},{4,6},{5,7},{6,4},{7,5},{8,10},{9,11},{10,... | collective-permute-start | bytes 2580488 | tf_op jit(solution)/shard_map/ppermute | solution.py:25
  199.8 39.9 %collective-permute-start.12 = (bf16[768,672]{0,1:T(8,128)(2,1)}, bf16[768,672]{0,1:T(8,128)(2,1)S(1)}, u32[]{:S(2)}, u32[]{:S(2)}) collective-permute-start(bf16[768,672]{0,1:T(8,128)(2,1)} %collective-permute-done.11), channel_id=1, source_target_pairs={{0,16},{16,0},{1,17},{17,1},{2,18},{18,2},{3,19},{19,3},{4,20},{20... | collective-permute-start | bytes 3096584 | tf_op jit(solution)/shard_map/ppermute | solution.py:25
  203.2 44.6 %collective-permute-start.14 = (bf16[768,672]{0,1:T(8,128)(2,1)S(1)}, bf16[768,672]{0,1:T(8,128)(2,1)S(1)}, u32[]{:S(2)}, u32[]{:S(2)}) collective-permute-start(bf16[768,672]{0,1:T(8,128)(2,1)S(1)} %fusion.24), channel_id=1, source_target_pairs={{0,16},{16,0},{1,17},{17,1},{2,18},{18,2},{3,19},{19,3},{4,20},{20... | collective-permute-start | bytes 3096584 | tf_op jit(solution)/shard_map/ppermute | solution.py:25
  223.9 25.7 %collective-permute-start.24 = (bf16[768,672]{0,1:T(8,128)(2,1)S(1)}, bf16[768,672]{0,1:T(8,128)(2,1)S(1)}, u32[]{:S(2)}, u32[]{:S(2)}) collective-permute-start(bf16[768,672]{0,1:T(8,128)(2,1)S(1)} %fusion.24), channel_id=1, source_target_pairs={{0,8},{4,12},{8,0},{12,4},{1,9},{5,13},{9,1},{13,5},{2,10},{6,14},... | collective-permute-start | bytes 3096584 | tf_op jit(solution)/shard_map/ppermute | solution.py:25
  238.1 28.1 %collective-permute-start.16 = (bf16[640,672]{0,1:T(8,128)(2,1)S(1)}, bf16[640,672]{0,1:T(8,128)(2,1)S(1)}, u32[]{:S(2)}, u32[]{:S(2)}) collective-permute-start(bf16[640,672]{0,1:T(8,128)(2,1)S(1)} %fusion.28), channel_id=1, source_target_pairs={{0,16},{16,0},{1,17},{17,1},{2,18},{18,2},{3,19},{19,3},{4,20},{20... | collective-permute-start | bytes 2580488 | tf_op jit(solution)/shard_map/ppermute | solution.py:25
  239.7 27.3 %collective-permute-start.26 = (bf16[640,672]{0,1:T(8,128)(2,1)S(1)}, bf16[640,672]{0,1:T(8,128)(2,1)S(1)}, u32[]{:S(2)}, u32[]{:S(2)}) collective-permute-start(bf16[640,672]{0,1:T(8,128)(2,1)S(1)} %fusion.28), channel_id=1, source_target_pairs={{0,8},{4,12},{8,0},{12,4},{1,9},{5,13},{9,1},{13,5},{2,10},{6,14},... | collective-permute-start | bytes 2580488 | tf_op jit(solution)/shard_map/ppermute | solution.py:25
  247.8 31.1 %collective-permute-start.17 = (bf16[512,672]{0,1:T(8,128)(2,1)S(1)}, bf16[512,672]{0,1:T(8,128)(2,1)S(1)}, u32[]{:S(2)}, u32[]{:S(2)}) collective-permute-start(bf16[512,672]{0,1:T(8,128)(2,1)S(1)} %fusion.33), channel_id=1, source_target_pairs={{0,2},{1,3},{2,0},{3,1},{4,6},{5,7},{6,4},{7,5},{8,10},{9,11},{10,... | collective-permute-start | bytes 2064392 | tf_op jit(solution)/shard_map/ppermute | solution.py:25
  249.6 38.7 %collective-permute-start.25 = (bf16[768,672]{0,1:T(8,128)(2,1)S(1)}, bf16[768,672]{0,1:T(8,128)(2,1)S(1)}, u32[]{:S(2)}, u32[]{:S(2)}) collective-permute-start(bf16[768,672]{0,1:T(8,128)(2,1)S(1)} %collective-permute-done.24), channel_id=1, source_target_pairs={{0,16},{16,0},{1,17},{17,1},{2,18},{18,2},{3,19},{19,3},{4,20},{20... | collective-permute-start | bytes 3096584 | tf_op jit(solution)/shard_map/ppermute | solution.py:25
  266.2 74.1 %collective-permute-start.20 = (bf16[1536,672]{0,1:T(8,128)(2,1)S(1)}, bf16[1536,672]{0,1:T(8,128)(2,1)S(1)}, u32[]{:S(2)}, u32[]{:S(2)}) collective-permute-start(bf16[1536,672]{0,1:T(8,128)(2,1)S(1)} %pad_maximum_fusion.2), channel_id=1, source_target_pairs={{0,4},{4,0},{8,12},{12,8},{1,5},{5,1},{9,13},{13,9},{2,6},{6,2},{1... | collective-permute-start | bytes 6193160 | tf_op jit(solution)/shard_map/ppermute | solution.py:25
  266.9 39.8 %collective-permute-start.27 = (bf16[640,672]{0,1:T(8,128)(2,1)S(1)}, bf16[640,672]{0,1:T(8,128)(2,1)S(1)}, u32[]{:S(2)}, u32[]{:S(2)}) collective-permute-start(bf16[640,672]{0,1:T(8,128)(2,1)S(1)} %collective-permute-done.26), channel_id=1, source_target_pairs={{0,16},{16,0},{1,17},{17,1},{2,18},{18,2},{3,19},{19,3},{4,20},{20... | collective-permute-start | bytes 2580488 | tf_op jit(solution)/shard_map/ppermute | solution.py:25
  279.1 41.4 %collective-permute-start.18 = (bf16[512,672]{0,1:T(8,128)(2,1)S(1)}, bf16[512,672]{0,1:T(8,128)(2,1)S(1)}, u32[]{:S(2)}, u32[]{:S(2)}) collective-permute-start(bf16[512,672]{0,1:T(8,128)(2,1)S(1)} %fusion.35), channel_id=1, source_target_pairs={{0,16},{16,0},{1,17},{17,1},{2,18},{18,2},{3,19},{19,3},{4,20},{20... | collective-permute-start | bytes 2064392 | tf_op jit(solution)/shard_map/ppermute | solution.py:25
  288.3 32.4 %collective-permute-start.28 = (bf16[512,672]{0,1:T(8,128)(2,1)S(1)}, bf16[512,672]{0,1:T(8,128)(2,1)S(1)}, u32[]{:S(2)}, u32[]{:S(2)}) collective-permute-start(bf16[512,672]{0,1:T(8,128)(2,1)S(1)} %fusion.35), channel_id=1, source_target_pairs={{0,8},{4,12},{8,0},{12,4},{1,9},{5,13},{9,1},{13,5},{2,10},{6,14},... | collective-permute-start | bytes 2064392 | tf_op jit(solution)/shard_map/ppermute | solution.py:25
  306.8 34.8 %collective-permute-start.21 = (bf16[1536,672]{0,1:T(8,128)(2,1)S(1)}, bf16[1536,672]{0,1:T(8,128)(2,1)S(1)}, u32[]{:S(2)}, u32[]{:S(2)}) collective-permute-start(bf16[1536,672]{0,1:T(8,128)(2,1)S(1)} %pad_maximum_fusion.4), channel_id=1, source_target_pairs={{0,4},{4,0},{8,12},{12,8},{1,5},{5,1},{9,13},{13,9},{2,6},{6,2},{1... | collective-permute-start | bytes 6193160 | tf_op jit(solution)/shard_map/ppermute | solution.py:25
  320.5 25.0 %collective-permute-start.31 = (bf16[1536,672]{0,1:T(8,128)(2,1)S(1)}, bf16[1536,672]{0,1:T(8,128)(2,1)S(1)}, u32[]{:S(2)}, u32[]{:S(2)}) collective-permute-start(bf16[1536,672]{0,1:T(8,128)(2,1)S(1)} %pad_maximum_fusion.3), channel_id=1, source_target_pairs={{0,4},{4,0},{8,12},{12,8},{1,5},{5,1},{9,13},{13,9},{2,6},{6,2},{1... | collective-permute-start | bytes 6193160 | tf_op jit(solution)/shard_map/ppermute | solution.py:25
  320.7 17.9 %collective-permute-start.29 = (bf16[512,672]{0,1:T(8,128)(2,1)S(1)}, bf16[512,672]{0,1:T(8,128)(2,1)S(1)}, u32[]{:S(2)}, u32[]{:S(2)}) collective-permute-start(bf16[512,672]{0,1:T(8,128)(2,1)S(1)} %collective-permute-done.28), channel_id=1, source_target_pairs={{0,16},{16,0},{1,17},{17,1},{2,18},{18,2},{3,19},{19,3},{4,20},{20... | collective-permute-start | bytes 2064392 | tf_op jit(solution)/shard_map/ppermute | solution.py:25
  338.7 8.4 %collective-permute-start.22 = (bf16[1280,672]{0,1:T(8,128)(2,1)S(1)}, bf16[1280,672]{0,1:T(8,128)(2,1)S(1)}, u32[]{:S(2)}, u32[]{:S(2)}) collective-permute-start(bf16[1280,672]{0,1:T(8,128)(2,1)S(1)} %pad_maximum_fusion.5), channel_id=1, source_target_pairs={{0,4},{4,0},{8,12},{12,8},{1,5},{5,1},{9,13},{13,9},{2,6},{6,2},{1... | collective-permute-start | bytes 5160968 | tf_op jit(solution)/shard_map/ppermute | solution.py:25
  339.7 11.0 %collective-permute-start.32 = (bf16[1536,672]{0,1:T(8,128)(2,1)S(1)}, bf16[1536,672]{0,1:T(8,128)(2,1)S(1)}, u32[]{:S(2)}, u32[]{:S(2)}) collective-permute-start(bf16[1536,672]{0,1:T(8,128)(2,1)S(1)} %constant_dynamic-update-slice_fusion), channel_id=1, source_target_pairs={{0,4},{4,0},{8,12},{12,8},{1,5},{5,1},{9,13},{13,9},{2,6},{6,2},{1... | collective-permute-start | bytes 6193160 | tf_op jit(solution)/shard_map/ppermute | solution.py:25
  (28 other events, 225.8 us)
Sparse Core Ops, SparseCore 0:
  361.5 51.3 reduce-scatter.3
